TPU v7x, 512 devices: a whole 4x8x8 slice. The times are simulated.
512 devices in a mesh: dp: 64 (over x, z, core), tensor: 8 (over y).
Axes of the slice: x: 4, y: 8, z: 8, core: 2. Of those that a mesh axis runs over, the one named last changes fastest.
Arguments:
- activations: bfloat16 [64, 1024, 5120], P('dp', 'tensor'), may hold values from -6 to 6
- out_grads: bfloat16 [64, 1024, 1024], P('dp', None, 'tensor'), may hold values from -0.1875 to 0.1875
- residual: bfloat16 [64, 5120, 1024], P('dp', None, 'tensor'), may hold values from -6 to 6
- q_start: float32 [1024, 32], P('tensor'), may hold values from -6 to 6
Outputs:
- p_factor: float32 [5120, 32], P('tensor')
- q_factor: float32 [1024, 32], P('tensor')
- residual_out: bfloat16 [64, 5120, 1024], P('dp', None, 'tensor')
All inputs are finite; a program needn't handle non-finite values.
Results may differ from a plain program's by a relative error of at most 0.0005.
Values may be sent and summed in bfloat16 or wider, within the bound.
No kernel may reach another device: no remote copies, remote signals or barrier semaphores. Data moves between devices by JAX's collectives and lax.ppermute only.
A program may use at most 64 MiB of HBM per device.

v0:
```python
import jax
import jax.numpy as jnp
from jax import lax
from jax.sharding import PartitionSpec as P


def orthonormal(left, gram):
    lower = jnp.linalg.cholesky(gram)
    return lax.linalg.triangular_solve(lower, left, left_side=False, lower=True, transpose_a=True)


def shards(activations, out_grads, residual, q_start):
    highest = lax.Precision.HIGHEST
    grads_local = out_grads[0]
    width = activations.shape[2]
    gradient = lax.dot_general(
        lax.all_gather(activations, "tensor", axis=1, tiled=True)[0],
        grads_local,
        (((0,), (0,)), ((), ())),
        preferred_element_type=jnp.float32,
    )
    merged = gradient + residual[0].astype(jnp.float32)
    local_left = jnp.dot(merged, q_start, precision=highest)
    p_sum = lax.psum(local_left, ("dp", "tensor"))
    basis = orthonormal(p_sum, jnp.dot(p_sum.T, p_sum, precision=highest))
    right_local = lax.dot_general(
        merged,
        basis,
        (((0,), (0,)), ((), ())),
        precision=highest,
        preferred_element_type=jnp.float32,
    )
    q_sum = lax.psum(right_local, "dp")
    q_factor = q_sum / lax.axis_size("dp")
    residual_out = (merged - jnp.dot(basis, q_factor.T, precision=highest)).astype(jnp.bfloat16)[
        None
    ]
    own_rows = width // lax.axis_size("tensor")
    p_factor = lax.dynamic_slice_in_dim(
        basis, lax.axis_index("tensor") * own_rows, own_rows, 0
    ) * jnp.sqrt(jnp.float32(width))
    return (p_factor, q_factor, residual_out)


def solution(mesh):
    return jax.shard_map(
        shards,
        mesh=mesh,
        in_specs=(
            P("dp", "tensor", None),
            P("dp", None, "tensor"),
            P("dp", None, "tensor"),
            P("tensor", None),
        ),
        out_specs=(P("tensor", None), P("tensor", None), P("dp", None, "tensor")),
        check_vma=False,
    )
```

profile of v0, /device:TPU:1, one launch (start us, length us, event | category | flops | bytes accessed | tf_op | source)
XLA Modules:
  0.0 682.0 jit_solution(459310928335990369)
XLA Ops:
  7.2 0.0 copy-start
  7.2 0.0 all-gather.2.cloned.1.call-start
  7.2 0.7 all-gather.2.cloned.1.call-update
  7.9 0.0 copy-start.2
  7.9 0.0 all-reduce.2.cloned.1.call-start
  8.0 123.8 %all-gather.2.cloned.1.call-done = bf16[1,1024,5120]{2,1,0:T(8,128)(2,1)} async-done(((bf16[1,128,5120]{2,1,0:T(8,128)(2,1)}), bf16[1,1024,5120]{2,1,0:T(8,128)(2,1)}) %all-gather.2.cloned.1.call-update) | async-done | bytes 10485776 | tf_op jit(solution)/shard_map/all_gather | solution.py:17
  131.7 0.0 copy-done
  131.7 7.2 %fusion.2 = f32[5120,128]{1,0:T(8,128)S(1)} fusion(bf16[1,1024,5120]{2,1,0:T(8,128)(2,1)} %all-gather.2.cloned.1.call-done, bf16[1,5120,128]{2,1,0:T(8,128)(2,1)} %param.6, bf16[1,1024,128]{2,1,0:T(8,128)(2,1)S(1)} %copy-done), kind=kOutput, calls=%fused_computation.3 | convolution fusion | flops 1343488000 | bytes 14680064 | tf_op jit(solution)/shard_map/dot_general | solution.py:16
  139.0 0.0 copy-done.2
  139.0 3.5 fusion.12
  142.5 0.0 all-reduce.2.cloned.1.call-update
  142.6 270.3 %all-reduce.2.cloned.1.call-done = f32[5120,32]{0,1:T(8,128)} async-done(((f32[5120,32]{0,1:T(8,128)}), f32[5120,32]{0,1:T(8,128)}) %all-reduce.2.cloned.1.call-update) | async-done | bytes 655376 | tf_op jit(solution)/shard_map/psum | solution.py:24
  412.9 1.9 fusion.13
  414.8 0.1 copy.7
  414.9 2.9 cholesky.16
  417.8 0.6 compare_reduce_fusion
  418.5 0.7 fusion.8
  419.1 2.4 custom-call.6
  421.6 1.8 fusion.9
  423.4 1.6 fusion.14
  425.0 243.4 %psum.15 = f32[128,32]{0,1:T(8,128)} all-reduce(f32[128,32]{0,1:T(8,128)S(1)} %fusion.14), channel_id=1, replica_groups=mesh['dp'=64,'tensor'=8] {'dp'}, use_global_device_ids=true, to_apply=%region_3.4 | all-reduce | flops 4096 | bytes 32768 | tf_op jit(solution)/shard_map/psum | solution.py:33
  668.5 0.7 broadcast_multiply_fusion
  669.2 0.0 copy-start.1
  669.2 5.3 fusion.6
  674.5 0.6 dynamic-slice_multiply_fusion
  675.1 0.0 copy-done.1
  (2 shorter events, 0.0 us)
Async XLA Ops:
  7.2 124.6 %copy-start = (bf16[1,1024,128]{2,1,0:T(8,128)(2,1)S(1)}, bf16[1,1024,128]{2,1,0:T(8,128)(2,1)}, u32[]{:S(2)}) copy-start(bf16[1,1024,128]{2,1,0:T(8,128)(2,1)} %param.5) | copy-start | bytes 786436
  7.2 124.6 %all-gather.2.cloned.1.call-start = ((), (), s32[]{:S(2)}) async-start(), calls=%async_computation | async-start | bytes 11796480 | tf_op jit(solution)/shard_map/all_gather | solution.py:17
  7.9 131.1 %copy-start.2 = (f32[128,32]{0,1:T(8,128)S(1)}, f32[128,32]{0,1:T(8,128)}, u32[]{:S(2)}) copy-start(f32[128,32]{0,1:T(8,128)} %param.7) | copy-start | bytes 49156
  7.9 404.9 %all-reduce.2.cloned.1.call-start = ((), (), s32[]{:S(2)}) async-start(), calls=%async_computation.1 | async-start | bytes 1310720 | tf_op jit(solution)/shard_map/psum | solution.py:24
  669.2 6.0 copy-start.1
Sparse Core Ops, SparseCore 0:
  10.1 121.5 all-gather.1
  142.7 270.1 all-reduce.1
where the time goes:
time: 688 us; the launch traced here: 682 us
  waiting for transfers between devices  395 us (57%)
  blocking collectives  243 us (35%)
  matrix products  21.5 us (3%)
  between operations  14.1 us (2%)
  other arithmetic  8.05 us (1%)
    psum x1, waiting for transfers between devices, shards(): p_sum = lax.psum(local_left, ('dp', 'tensor'))  270 us
    psum x1, blocking collectives, shards(): q_sum = lax.psum(right_local, 'dp')  243 us
    all_gather x1, waiting for transfers between devices, shards(): lax.all_gather(activations, 'tensor', axis=1, tiled=True)[0]  124 us
  transfers between devices with their start and end apart: 2, of which 2 were waited for; matrix products, arithmetic and copies ran while one was open for 0% of the time, Pallas kernels for 0%

commit v1 on v0

v1 whole, which is shorter than its diff:
```python
import jax
import jax.numpy as jnp
from jax import lax
from jax.experimental import pallas as pl
from jax.experimental.pallas import tpu as pltpu
from jax.sharding import Mesh
from jax.sharding import PartitionSpec as P

F32 = jnp.float32
BF16 = jnp.bfloat16
NN = (((1,), (0,)), ((), ()))
NT = (((1,), (1,)), ((), ()))
VMEM = pl.BlockSpec(memory_space=pltpu.VMEM)
SMEM = pl.BlockSpec(memory_space=pltpu.SMEM)
XZ = ("x", "z")
COLUMN_BLOCK = 640


def call(kernel, outs, flops, moved):
    several = isinstance(outs, list)
    shapes = [jax.ShapeDtypeStruct(*o) for o in (outs if several else [outs])]

    def run(*operands, scratch=(), smem=()):
        return pl.pallas_call(
            kernel,
            out_shape=shapes if several else shapes[0],
            in_specs=[SMEM if i in smem else VMEM for i in range(len(operands))],
            out_specs=[VMEM] * len(shapes) if several else VMEM,
            scratch_shapes=list(scratch),
            compiler_params=pltpu.CompilerParams(vmem_limit_bytes=40 * 1024 * 1024),
            cost_estimate=pl.CostEstimate(flops=flops, bytes_accessed=moved, transcendentals=0),
        )(*operands)

    return run


def pieces(x):
    high = x.astype(BF16)
    rest = x - high.astype(F32)
    middle = rest.astype(BF16)
    low = (rest - middle.astype(F32)).astype(BF16)
    return high, middle, low


def stacked(x):
    return jnp.concatenate(pieces(x), axis=0)


def folded(y):
    n = y.shape[0] // 3
    return y[:n] + (y[n : 2 * n] + y[2 * n :])


def dot(a, b, dims):
    return lax.dot_general(a, b, dims, preferred_element_type=F32)


def token_terms(q_ref, grads_ref, out_ref):
    q3 = stacked(q_ref[...])
    parts, _, tokens = out_ref.shape
    for j in range(parts):
        out_ref[j] = folded(dot(q3, grads_ref[pl.ds(j * tokens, tokens), :], NT))


def residual_left(q_ref, residual_ref, out_ref):
    q3 = stacked(q_ref[...])
    for b in range(0, out_ref.shape[1], COLUMN_BLOCK):
        block = pl.ds(b, COLUMN_BLOCK)
        out_ref[:, block] = folded(dot(q3, residual_ref[block, :], NT))


def left_terms(tokens_ref, acts_ref, base_ref, out_ref):
    z = tokens_ref[0]
    for j in range(1, tokens_ref.shape[0]):
        z = z + tokens_ref[j]
    z3 = stacked(z)
    half = out_ref.shape[1]
    for b in range(0, out_ref.shape[2], COLUMN_BLOCK):
        block = pl.ds(b, COLUMN_BLOCK)
        left = folded(dot(z3, acts_ref[:, block], NN)) + base_ref[:, block]
        out_ref[0, :, block] = left[:half]
        out_ref[1, :, block] = left[half:]


def cut_left(halves_ref, out_ref):
    chunks, rows, width = out_ref.shape
    groups = halves_ref.shape[1] // rows
    per = chunks // groups
    for g in range(groups):
        for i in range(0, per, 2):
            both = pl.ds(i * width, 2 * width)
            here = pl.ds(g * rows, rows)
            total = halves_ref[0, here, both] + halves_ref[1, here, both]
            out_ref[g * per + i] = total[:, :width]
            out_ref[g * per + i + 1] = total[:, width:]


def sum_and_fan(in_ref, out_ref):
    total = in_ref[0]
    for j in range(1, in_ref.shape[0]):
        total = total + in_ref[j]
    for j in range(out_ref.shape[0]):
        out_ref[j] = total


def inverse_factor(gram, n):
    row_at = lax.broadcasted_iota(jnp.int32, (n, 2 * n), 0)
    col_at = lax.broadcasted_iota(jnp.int32, (n, 2 * n), 1)
    unit = (col_at == row_at + n).astype(F32)
    work = jnp.concatenate([gram, unit[:, n:]], axis=1)
    scale = jnp.zeros((n, 1), F32)
    rows_only = row_at[:, :1]
    for k in range(n):
        pivot = work[k : k + 1, k : k + 1]
        scale = jnp.where(rows_only == k, pivot, scale)
        if k < n - 1:
            factor = work[:, k : k + 1] / pivot
            factor = jnp.where(rows_only > k, factor, 0.0)
            work = work - factor * work[k : k + 1, :]
    return work[:, n:] / jnp.sqrt(scale)


def orthonormal(core_ref, own_ref, other_ref, acts_ref, basis_ref, basis3_ref, tokens_ref, left, left3):
    n, width = left.shape
    rows = own_ref.shape[1]
    step = own_ref.shape[2]
    groups = n // (2 * rows)
    per = width // step
    first = core_ref[0] == 0
    for g in range(groups):
        for i in range(0, per, 2):
            at = g * per + i
            mine = jnp.concatenate([own_ref[at], own_ref[at + 1]], axis=1)
            theirs = jnp.concatenate([other_ref[at], other_ref[at + 1]], axis=1)
            both = pl.ds(i * step, 2 * step)
            left[pl.ds(g * rows, rows), both] = jnp.where(first, mine, theirs)
            left[pl.ds(n // 2 + g * rows, rows), both] = jnp.where(first, theirs, mine)
    nine = jnp.zeros((3 * n, 3 * n), F32)
    for b in range(0, width, COLUMN_BLOCK):
        block = pl.ds(b, COLUMN_BLOCK)
        l3 = stacked(left[:, block])
        left3[:, block] = l3
        nine = nine + dot(l3, l3, NT)
    part = lambda i, j: nine[i * n : (i + 1) * n, j * n : (j + 1) * n]
    gram = part(0, 0) + (
        (part(0, 1) + part(1, 0)) + ((part(0, 2) + part(2, 0) + part(1, 1)) + ((part(1, 2) + part(2, 1)) + part(2, 2)))
    )
    high, middle, low = pieces(inverse_factor(gram, n))
    wide = jnp.concatenate([high, high, high, middle, middle, low], axis=1)
    terms = jnp.zeros((3 * n, acts_ref.shape[0]), F32)
    for b in range(0, width, COLUMN_BLOCK):
        block = pl.ds(b, COLUMN_BLOCK)
        l3 = left3[:, block]
        tall = jnp.concatenate([l3, l3[: 2 * n], l3[:n]], axis=0)
        basis = dot(wide, tall, NN)
        basis_ref[:, block] = basis
        b3 = stacked(basis)
        basis3_ref[:, block] = b3
        terms = terms + dot(b3, acts_ref[:, block], NT)
    terms = folded(terms)
    for j in range(tokens_ref.shape[0]):
        tokens_ref[j] = terms


def residual_right(basis3_ref, residual_ref, out_ref, tall_ref):
    n = out_ref.shape[0]
    total = jnp.zeros((3 * n, out_ref.shape[1]), F32)
    for b in range(0, basis3_ref.shape[1], COLUMN_BLOCK):
        block = pl.ds(b, COLUMN_BLOCK)
        b3 = basis3_ref[:, block]
        total = total + dot(b3, residual_ref[block, :], NN)
        six = jnp.concatenate([b3, b3[: 2 * n], b3[:n]], axis=0)
        tall_ref[block, :] = six.T
    out_ref[...] = folded(total)


def right_terms(tokens_ref, base_ref, grads_ref, out_ref):
    total = base_ref[...]
    tokens = tokens_ref.shape[2]
    for j in range(tokens_ref.shape[0]):
        total = total + folded(dot(stacked(tokens_ref[j]), grads_ref[pl.ds(j * tokens, tokens), :], NN))
    half = out_ref.shape[1]
    out_ref[0] = total[:half]
    out_ref[1] = total[half:]


def sum_right(in_ref, out_ref):
    total = in_ref[0]
    for j in range(1, in_ref.shape[0]):
        total = total + in_ref[j]
    out_ref[...] = total


def finish(core_ref, scale_ref, own_ref, other_ref, merged_ref, tall_ref, right_ref, residual_ref):
    first = core_ref[0] == 0
    own, other = own_ref[...], other_ref[...]
    right = jnp.concatenate([jnp.where(first, own, other), jnp.where(first, other, own)], axis=0)
    right = right * scale_ref[0]
    right_ref[...] = right
    high, middle, low = pieces(right)
    six = jnp.concatenate([high, high, high, middle, middle, low], axis=0)
    for b in range(0, merged_ref.shape[0], COLUMN_BLOCK):
        block = pl.ds(b, COLUMN_BLOCK)
        residual_ref[block, :] = (merged_ref[block, :] - dot(tall_ref[block, :], six, NN)).astype(BF16)


def shards(activations, out_grads, residual, q_start):
    acts, grads, resid = activations[0], out_grads[0], residual[0]
    own_tokens, width = acts.shape
    all_tokens, columns = grads.shape
    rank = q_start.shape[1]
    nt, nxz = lax.axis_size("tensor"), lax.axis_size(XZ)
    replicas = lax.axis_size(("x", "z", "core"))
    half = rank // 2
    chunk = half * width // (8 * nxz)
    core = lax.axis_index("core").astype(jnp.int32).reshape(1)
    swap = [(0, 1), (1, 0)]
    qt = q_start.T

    with jax.named_scope("gather_activations"):
        gathered = lax.all_gather(acts, "tensor", axis=0, tiled=True)

    with jax.named_scope("token_terms"):
        z = call(token_terms, ((nt, rank, own_tokens), F32), 2 * 3 * rank * columns * all_tokens, 2**19)(qt, grads)
        z = lax.all_to_all(z, "tensor", 0, 0)
    with jax.named_scope("residual_left"):
        base = call(residual_left, ((rank, width), F32), 2 * 3 * rank * columns * width, 2**21)(qt, resid)
    with jax.named_scope("left_terms"):
        left = call(left_terms, ((2, half, width), F32), 2 * 3 * rank * own_tokens * width, 2**22)(z, acts, base)
    with jax.named_scope("left_sum"):
        left = lax.all_to_all(left, "core", 0, 0)
        left = call(cut_left, ((nxz, 8, chunk), F32), 2**18, 2**20)(left)
        left = lax.all_to_all(left, XZ, 0, 0)
        left = call(sum_and_fan, ((nt, 8, chunk), F32), 2**18, 2**19)(left)
        left = lax.all_to_all(left, "tensor", 0, 0)
        left = call(sum_and_fan, ((nxz, 8, chunk), F32), 2**18, 2**19)(left)
        own = lax.all_to_all(left, XZ, 0, 0)
        other = lax.ppermute(own, "core", swap)
    with jax.named_scope("orthonormal"):
        basis, basis3, tokens = call(
            orthonormal,
            [((rank, width), F32), ((3 * rank, width), BF16), ((nt, rank, own_tokens), F32)],
            2 * 9 * rank * rank * width,
            2**22,
        )(
            core,
            own,
            other,
            acts,
            scratch=(pltpu.VMEM((rank, width), F32), pltpu.VMEM((3 * rank, width), BF16)),
            smem=(0,),
        )
        tokens = lax.all_to_all(tokens, "tensor", 0, 0)
    with jax.named_scope("residual_right"):
        base, tall = call(
            residual_right, [((rank, columns), F32), ((width, 6 * rank), BF16)], 2 * 3 * rank * columns * width, 2**22
        )(basis3, resid)
    with jax.named_scope("right_terms"):
        right = call(right_terms, ((2, half, columns), F32), 2 * 3 * rank * all_tokens * columns, 2**19)(
            tokens, base, grads
        )
    with jax.named_scope("right_sum"):
        right = lax.all_to_all(right, "core", 0, 0)
        fan = call(sum_and_fan, ((nxz, half, columns), F32), 2**16, 2**18)(right)
        right = lax.all_to_all(fan, XZ, 0, 0)
        own = call(sum_right, ((half, columns), F32), 2**16, 2**18)(right)
        other = lax.ppermute(own, "core", swap)
    with jax.named_scope("merged"):
        gathered, _ = lax.optimization_barrier((gathered, fan))
        merged = lax.dot_general(
            gathered, grads, (((0,), (0,)), ((), ())), preferred_element_type=F32
        ) + resid.astype(F32)
    with jax.named_scope("finish"):
        right, residual_out = call(
            finish, [((rank, columns), F32), ((width, columns), BF16)], 2 * 6 * rank * width * columns, 2**22
        )(core, jnp.full((1,), 1.0 / replicas, F32), own, other, merged, tall, smem=(0, 1))
    with jax.named_scope("p_factor"):
        own_rows = width // nt
        p_factor = lax.dynamic_slice_in_dim(basis, lax.axis_index("tensor") * own_rows, own_rows, 1).T
        p_factor = p_factor * jnp.sqrt(jnp.float32(width))
    return (p_factor, right.T, residual_out[None])


def solution(mesh):
    replicas, tensor = mesh.devices.shape
    zs = 8
    fine = Mesh(mesh.devices.reshape(replicas // (2 * zs), zs, 2, tensor), ("x", "z", "core", "tensor"))
    dp = ("x", "z", "core")
    return jax.shard_map(
        shards,
        mesh=fine,
        in_specs=(
            P(dp, "tensor", None),
            P(dp, None, "tensor"),
            P(dp, None, "tensor"),
            P("tensor", None),
        ),
        out_specs=(P("tensor", None), P("tensor", None), P(dp, None, "tensor")),
        check_vma=False,
    )
```

time: 688 us -> 159 us (0.23)
  waiting for transfers between devices: 395 us -> 23.9 us
  blocking collectives: 243 us -> 64.4 us
  starting transfers between devices: 0.08 us -> 28.4 us
  matrix products: 21.5 us -> 5.8 us
  Pallas kernels: 0 us -> 12.5 us
  local copies, waits for them, and re-layouts: 0.09 us -> 6.99 us
    psum x1 -> x0, waiting for transfers between devices: 270 us -> none  [shards(): p_sum = lax.psum(local_left, ('dp', 'tensor'))]
    psum x1 -> x0, blocking collectives: 243 us -> none  [shards(): q_sum = lax.psum(right_local, 'dp')]
    all_gather x1, waiting for transfers between devices: 124 us -> 0.02 us  [shards(): gathered = lax.all_gather(acts, 'tensor', axis=0, tiled=True)]
    all_to_all x0 -> x5, blocking collectives: none -> 64.4 us  [the longest x1 22.9 us: shards(): left = lax.all_to_all(left, XZ, 0, 0)]
    all_to_all x0 -> x3, waiting for transfers between devices: none -> 21.8 us  [the longest x1 8.14 us: shards(): right = lax.all_to_all(fan, XZ, 0, 0)]
    all_to_all x0 -> x3, starting transfers between devices: none -> 15.9 us  [the longest x1 7.65 us: shards(): z = lax.all_to_all(z, 'tensor', 0, 0)]
    dot_general x5 -> x1, matrix products: 19.6 us -> 5.8 us  [shards(): lax.dot_general(gathered, grads, (((0,), (0,)), ((), ())), preferred_elem...]
    pallas_call x0 -> x12, Pallas kernels: none -> 12.5 us  [run(): pl.pallas_call(kernel, out_shape=shapes if several else shapes[0], in_spe...]
  transfers between devices with their start and end apart: 2 -> 6, of which waited for: 2 -> 4; matrix products, arithmetic and copies ran while one was open for 0% -> 5% of each run, Pallas kernels for 0% -> 7%
where the time goes in v1:
time: 159 us; the launch traced here: 158 us
  blocking collectives  64.4 us (41%)
  starting transfers between devices  28.4 us (18%)
  waiting for transfers between devices  23.9 us (15%)
  between operations  14.2 us (9%)
  Pallas kernels  12.5 us (8%)
  local copies, waits for them, and re-layouts  6.99 us (4%)
  matrix products  5.8 us (4%)
    all_to_all x1, blocking collectives, shards(): left = lax.all_to_all(left, XZ, 0, 0)  22.9 us
    all_to_all x1, blocking collectives, shards(): own = lax.all_to_all(left, XZ, 0, 0)  18.5 us
    pallas_call x12, Pallas kernels, run(): pl.pallas_call(kernel, out_shape=shapes if several else shapes[0], in_spe...  12.5 us
    ppermute x2, starting transfers between devices, shards(): other = lax.ppermute(own, 'core', swap)  12.4 us
    all_to_all x1, blocking collectives, shards(): left = lax.all_to_all(left, 'tensor', 0, 0)  11 us
    all_to_all x1, waiting for transfers between devices, shards(): right = lax.all_to_all(fan, XZ, 0, 0)  8.14 us
    all_to_all x1, starting transfers between devices, shards(): z = lax.all_to_all(z, 'tensor', 0, 0)  7.65 us
    all_to_all x1, blocking collectives, shards(): left = lax.all_to_all(left, 'core', 0, 0)  7.46 us
  transfers between devices with their start and end apart: 6, of which 4 were waited for; matrix products, arithmetic and copies ran while one was open for 5% of the time, Pallas kernels for 7%

profile of v1, /device:TPU:1, one launch (start us, length us, event | category | flops | bytes accessed | tf_op | source)
XLA Modules:
  0.0 157.7 jit_solution(13765178387522457164)
XLA Ops:
  7.2 0.7 all-gather.3.cloned.1.call-update
  7.9 1.0 copy-done.4
  8.9 0.7 copy-done.8
  9.6 0.9 token_terms.1
  10.6 7.7 %all-to-all-start = ((f32[8,32,128]{2,1,0:T(8,128)}), f32[8,32,128]{2,1,0:T(8,128)S(1)}, u32[]{:S(2)}, u32[]{:S(2)}) async-start(f32[8,32,128]{2,1,0:T(8,128)} %token_terms.1), calls=%async_computation | async-start | bytes 262144 | tf_op jit(solution)/shard_map/token_terms/all_to_all | solution.py:225
  18.2 0.7 copy-done.9
  18.9 0.6 residual_left.1.base_ref
  19.5 6.7 %all-to-all-done.tokens_ref = f32[8,32,128]{2,1,0:T(8,128)S(1)} async-done(((f32[8,32,128]{2,1,0:T(8,128)}), f32[8,32,128]{2,1,0:T(8,128)S(1)}, u32[]{:S(2)}, u32[]{:S(2)}) %all-to-all-start) | async-done | bytes 131104 | tf_op jit(solution)/shard_map/token_terms/all_to_all | solution.py:225
  26.2 0.4 left_terms.1
  26.7 7.5 %all_to_all.40.halves_ref = f32[2,16,5120]{2,1,0:T(8,128)S(1)} all-to-all(f32[2,16,5120]{2,1,0:T(8,128)S(1)} %left_terms.1), channel_id=1, replica_groups=mesh['x'=4,'z'=8,'core'=2,'tensor'=8] {'core'}, dimensions={0} | all-to-all | bytes 1310720 | tf_op jit(solution)/shard_map/left_sum/all_to_all | solution.py:231
  34.3 22.9 %all_to_all.41.in_ref = f32[32,8,320]{2,1,0:T(8,128)S(1)} all-to-all(f32[32,8,320]{2,1,0:T(8,128)S(1)} %left_sum.3), channel_id=1, replica_groups=mesh['x'=4,'z'=8,'core'=2,'tensor'=8] {'x','z'}, dimensions={0} | all-to-all | bytes 655360 | tf_op jit(solution)/shard_map/left_sum/all_to_all | solution.py:233
  57.2 11.0 %all_to_all.42.in_ref = f32[8,8,320]{2,1,0:T(8,128)S(1)} all-to-all(f32[8,8,320]{2,1,0:T(8,128)S(1)} %left_sum.4), channel_id=1, replica_groups=mesh['x'=4,'z'=8,'core'=2,'tensor'=8] {'tensor'}, dimensions={0} | all-to-all | bytes 163840 | tf_op jit(solution)/shard_map/left_sum/all_to_all | solution.py:235
  68.3 18.5 %all_to_all.43.own_ref = f32[32,8,320]{2,1,0:T(8,128)S(1)} all-to-all(f32[32,8,320]{2,1,0:T(8,128)S(1)} %left_sum.5), channel_id=1, replica_groups=mesh['x'=4,'z'=8,'core'=2,'tensor'=8] {'x','z'}, dimensions={0} | all-to-all | bytes 655360 | tf_op jit(solution)/shard_map/left_sum/all_to_all | solution.py:237
  86.8 6.8 %collective-permute-start = (f32[32,8,320]{2,1,0:T(8,128)S(1)}, f32[32,8,320]{2,1,0:T(8,128)}, u32[]{:S(2)}, u32[]{:S(2)}) collective-permute-start(f32[32,8,320]{2,1,0:T(8,128)S(1)} %all_to_all.43.own_ref), channel_id=1, source_target_pairs={{0,8},{8,0},{1,9},{9,1},{2,10},{10,2},{3,11},{11,3},{4,12},{12,4},... | collective-permute-start | bytes 983048 | tf_op jit(solution)/shard_map/left_sum/ppermute | solution.py:238
  93.6 1.5 collective-permute-done.other_ref
  95.0 6.7 %orthonormal.1 = (f32[32,5120]{1,0:T(8,128)S(1)}, bf16[96,5120]{1,0:T(8,128)(2,1)S(1)}, f32[8,32,128]{2,1,0:T(8,128)}) custom-call(s32[1]{0:T(128)} %bitcast.core_ref, f32[32,8,320]{2,1,0:T(8,128)S(1)} %all_to_all.43.own_ref, f32[32,8,320]{2,1,0:T(8,128)} %collective-permute-done.other_ref, bf16[128,5120]{1,0:T(8,128)(2,1)S(1)} %bitcast.17), custom_call_target="tpu_custom_call" | custom-call | flops 94371840 | bytes 4194304 | tf_op jit(solution)/shard_map/orthonormal/pallas_call | solution.py:24
  101.7 0.9 copy-done.6
  102.7 0.8 copy-done.10
  103.5 3.4 %all-to-all-start.5 = ((f32[8,32,128]{2,1,0:T(8,128)}), f32[8,32,128]{2,1,0:T(8,128)S(1)}, u32[]{:S(2)}, u32[]{:S(2)}) async-start(f32[8,32,128]{2,1,0:T(8,128)} %get-tuple-element.12), calls=%async_computation.5 | async-start | bytes 262144 | tf_op jit(solution)/shard_map/orthonormal/all_to_all | solution.py:253
  106.9 1.2 copy-done.7
  108.1 0.8 residual_right.1
  108.9 1.6 %copy-done.2 = bf16[5120,192]{1,0:T(8,128)(2,1)} copy-done((bf16[5120,192]{1,0:T(8,128)(2,1)}, bf16[5120,192]{1,0:T(8,128)(2,1)S(1)}, u32[]{:S(2)}) %copy-start.2) | copy-done | bytes 1966104
  110.5 6.9 %all-to-all-done.5.tokens_ref = f32[8,32,128]{2,1,0:T(8,128)S(1)} async-done(((f32[8,32,128]{2,1,0:T(8,128)}), f32[8,32,128]{2,1,0:T(8,128)S(1)}, u32[]{:S(2)}, u32[]{:S(2)}) %all-to-all-start.5) | async-done | bytes 131104 | tf_op jit(solution)/shard_map/orthonormal/all_to_all | solution.py:253
  117.4 0.2 right_terms.1
  117.6 4.5 %all_to_all.44.in_ref = f32[2,16,128]{2,1,0:T(8,128)S(1)} all-to-all(f32[2,16,128]{2,1,0:T(8,128)S(1)} %right_terms.1), channel_id=1, replica_groups=mesh['x'=4,'z'=8,'core'=2,'tensor'=8] {'core'}, dimensions={0} | all-to-all | bytes 32768 | tf_op jit(solution)/shard_map/right_sum/all_to_all | solution.py:263
  122.1 0.7 right_sum.2
  122.8 4.9 %all-to-all-start.7 = ((f32[32,16,128]{2,1,0:T(8,128)}), f32[32,16,128]{2,1,0:T(8,128)S(1)}, u32[]{:S(2)}, u32[]{:S(2)}) async-start(f32[32,16,128]{2,1,0:T(8,128)} %right_sum.2), calls=%async_computation.7 | async-start | bytes 524288 | tf_op jit(solution)/shard_map/right_sum/all_to_all | solution.py:265
  127.7 1.5 multiply_bitcast_fusion
  129.3 8.1 %all-to-all-done.7.in_ref = f32[32,16,128]{2,1,0:T(8,128)S(1)} async-done(((f32[32,16,128]{2,1,0:T(8,128)}), f32[32,16,128]{2,1,0:T(8,128)S(1)}, u32[]{:S(2)}, u32[]{:S(2)}) %all-to-all-start.7) | async-done | bytes 262176 | tf_op jit(solution)/shard_map/right_sum/all_to_all | solution.py:265
  137.5 5.6 %collective-permute-start.1 = (f32[16,128]{1,0:T(8,128)S(1)}, f32[16,128]{1,0:T(8,128)S(1)}, u32[]{:S(2)}, u32[]{:S(2)}) collective-permute-start(f32[16,128]{1,0:T(8,128)S(1)} %right_sum.3.own_ref), channel_id=1, source_target_pairs={{0,8},{8,0},{1,9},{9,1},{2,10},{10,2},{3,11},{11,3},{4,12},{12,4},... | collective-permute-start | bytes 24584 | tf_op jit(solution)/shard_map/right_sum/ppermute | solution.py:267
  143.1 5.8 %convolution_add_fusion.merged_ref = f32[5120,128]{1,0:T(8,128)S(1)} fusion(bf16[1024,5120]{1,0:T(8,128)(2,1)} %bitcast.22, bf16[1,5120,128]{2,1,0:T(8,128)(2,1)S(1)} %copy-done, bf16[1,1024,128]{2,1,0:T(8,128)(2,1)S(1)} %copy-done.5), kind=kOutput, calls=%fused_computation | convolution fusion | flops 1343488000 | bytes 14680064 | tf_op jit(solution)/shard_map/merged/dot_general | solution.py:270
  148.9 1.9 %finish.1 = (f32[32,128]{1,0:T(8,128)}, bf16[5120,128]{1,0:T(8,128)(2,1)}) custom-call(s32[1]{0:T(128)} %bitcast.core_ref, f32[1]{0:T(128)} %constant.18.clone.1.scale_ref, f32[16,128]{1,0:T(8,128)S(1)} %right_sum.3.own_ref, f32[16,128]{1,0:T(8,128)S(1)} %collective-permute-done.1.other_ref, f32[5120,128]{1,0:T(8,128)S(1)} %convolution_add_fusion.merged_ref, ...), custom_call_target="tpu_custom_call" | custom-call | flops 251658240 | bytes 4194304 | tf_op jit(solution)/shard_map/finish/pallas_call | solution.py:24
  (22 shorter events, 0.3 us)
Async XLA Ops:
  7.2 11.0 %copy-start = (bf16[1,5120,128]{2,1,0:T(8,128)(2,1)S(1)}, bf16[1,5120,128]{2,1,0:T(8,128)(2,1)}, u32[]{:S(2)}) copy-start(bf16[1,5120,128]{2,1,0:T(8,128)(2,1)} %param.6) | copy-start | bytes 3932164
  7.2 19.1 %copy-start.1 = (bf16[1,128,5120]{2,1,0:T(8,128)(2,1)S(1)}, bf16[1,128,5120]{2,1,0:T(8,128)(2,1)}, u32[]{:S(2)}) copy-start(bf16[1,128,5120]{2,1,0:T(8,128)(2,1)} %param.4) | copy-start | bytes 3932164
  7.2 135.9 %all-gather.3.cloned.1.call-start = ((), (), s32[]{:S(2)}) async-start(), calls=%async_computation.8 | async-start | bytes 11796480 | tf_op jit(solution)/shard_map/gather_activations/all_gather | solution.py:221
  7.9 1.0 copy-start.4
  8.9 0.7 copy-start.8
  10.6 15.7 %all-to-all-start = ((f32[8,32,128]{2,1,0:T(8,128)}), f32[8,32,128]{2,1,0:T(8,128)S(1)}, u32[]{:S(2)}, u32[]{:S(2)}) async-start(f32[8,32,128]{2,1,0:T(8,128)} %token_terms.1), calls=%async_computation | async-start | bytes 262144 | tf_op jit(solution)/shard_map/token_terms/all_to_all | solution.py:225
  18.2 0.7 copy-start.9
  68.3 49.1 %copy-start.5 = (bf16[1,1024,128]{2,1,0:T(8,128)(2,1)S(1)}, bf16[1,1024,128]{2,1,0:T(8,128)(2,1)}, u32[]{:S(2)}) copy-start(bf16[1,1024,128]{2,1,0:T(8,128)(2,1)} %param.5) | copy-start | bytes 786436
  86.8 8.3 %collective-permute-start = (f32[32,8,320]{2,1,0:T(8,128)S(1)}, f32[32,8,320]{2,1,0:T(8,128)}, u32[]{:S(2)}, u32[]{:S(2)}) collective-permute-start(f32[32,8,320]{2,1,0:T(8,128)S(1)} %all_to_all.43.own_ref), channel_id=1, source_target_pairs={{0,8},{8,0},{1,9},{9,1},{2,10},{10,2},{3,11},{11,3},{4,12},{12,4},... | collective-permute-start | bytes 983048 | tf_op jit(solution)/shard_map/left_sum/ppermute | solution.py:238
  101.7 0.9 copy-start.6
  102.7 0.8 copy-start.10
  103.5 13.9 %all-to-all-start.5 = ((f32[8,32,128]{2,1,0:T(8,128)}), f32[8,32,128]{2,1,0:T(8,128)S(1)}, u32[]{:S(2)}, u32[]{:S(2)}) async-start(f32[8,32,128]{2,1,0:T(8,128)} %get-tuple-element.12), calls=%async_computation.5 | async-start | bytes 262144 | tf_op jit(solution)/shard_map/orthonormal/all_to_all | solution.py:253
  106.9 1.2 copy-start.7
  108.9 1.6 %copy-start.2 = (bf16[5120,192]{1,0:T(8,128)(2,1)}, bf16[5120,192]{1,0:T(8,128)(2,1)S(1)}, u32[]{:S(2)}) copy-start(bf16[5120,192]{1,0:T(8,128)(2,1)S(1)} %get-tuple-element.16.tall_ref) | copy-start | bytes 5898244
  122.8 14.6 %all-to-all-start.7 = ((f32[32,16,128]{2,1,0:T(8,128)}), f32[32,16,128]{2,1,0:T(8,128)S(1)}, u32[]{:S(2)}, u32[]{:S(2)}) async-start(f32[32,16,128]{2,1,0:T(8,128)} %right_sum.2), calls=%async_computation.7 | async-start | bytes 524288 | tf_op jit(solution)/shard_map/right_sum/all_to_all | solution.py:265
  137.5 11.5 %collective-permute-start.1 = (f32[16,128]{1,0:T(8,128)S(1)}, f32[16,128]{1,0:T(8,128)S(1)}, u32[]{:S(2)}, u32[]{:S(2)}) collective-permute-start(f32[16,128]{1,0:T(8,128)S(1)} %right_sum.3.own_ref), channel_id=1, source_target_pairs={{0,8},{8,0},{1,9},{9,1},{2,10},{10,2},{3,11},{11,3},{4,12},{12,4},... | collective-permute-start | bytes 24584 | tf_op jit(solution)/shard_map/right_sum/ppermute | solution.py:267
  143.1 5.8 %copy-start.3 = (bf16[5120,192]{1,0:T(8,128)(2,1)S(1)}, bf16[5120,192]{1,0:T(8,128)(2,1)}, u32[]{:S(2)}) copy-start(bf16[5120,192]{1,0:T(8,128)(2,1)} %copy-done.2) | copy-start | bytes 5898244
Sparse Core Ops, SparseCore 0:
  10.1 126.5 all-gather.2

commit v2 on v1

v2 whole, which is shorter than its diff:
```python
import jax
import jax.numpy as jnp
from jax import lax
from jax.experimental import pallas as pl
from jax.experimental.pallas import tpu as pltpu
from jax.sharding import Mesh
from jax.sharding import PartitionSpec as P

F32 = jnp.float32
BF16 = jnp.bfloat16
NN = (((1,), (0,)), ((), ()))
NT = (((1,), (1,)), ((), ()))
VMEM = pl.BlockSpec(memory_space=pltpu.VMEM)
SMEM = pl.BlockSpec(memory_space=pltpu.SMEM)
XZ = ("x", "z")
COLUMN_BLOCK = 640
ROW_BLOCK = 2560


def call(kernel, outs, flops, moved):
    several = isinstance(outs, list)
    shapes = [jax.ShapeDtypeStruct(*o) for o in (outs if several else [outs])]

    def run(*operands, scratch=(), smem=()):
        return pl.pallas_call(
            kernel,
            out_shape=shapes if several else shapes[0],
            in_specs=[SMEM if i in smem else VMEM for i in range(len(operands))],
            out_specs=[VMEM] * len(shapes) if several else VMEM,
            scratch_shapes=list(scratch),
            compiler_params=pltpu.CompilerParams(vmem_limit_bytes=16 * 1024 * 1024),
            cost_estimate=pl.CostEstimate(flops=flops, bytes_accessed=moved, transcendentals=0),
        )(*operands)

    return run


def pieces(x):
    high = x.astype(BF16)
    rest = x - high.astype(F32)
    middle = rest.astype(BF16)
    low = (rest - middle.astype(F32)).astype(BF16)
    return high, middle, low


def stacked(x):
    return jnp.concatenate(pieces(x), axis=0)


def folded(y):
    n = y.shape[0] // 3
    return y[:n] + (y[n : 2 * n] + y[2 * n :])


def six_left(x):
    high, middle, low = pieces(x)
    return jnp.concatenate([high, high, high, middle, middle, low], axis=1)


def six_right(x):
    high, middle, low = pieces(x)
    return jnp.concatenate([high, middle, low, high, middle, high], axis=0)


def dot(a, b, dims):
    return lax.dot_general(a, b, dims, preferred_element_type=F32)


def token_terms(q_ref, grads_ref, out_ref):
    q3 = stacked(q_ref[...])
    parts, _, tokens = out_ref.shape
    for j in range(parts):
        out_ref[j] = folded(dot(q3, grads_ref[pl.ds(j * tokens, tokens), :], NT))


def residual_left(q_ref, residual_ref, out_ref):
    q3 = stacked(q_ref[...])
    for b in range(0, out_ref.shape[1], COLUMN_BLOCK):
        block = pl.ds(b, COLUMN_BLOCK)
        out_ref[:, block] = folded(dot(q3, residual_ref[block, :], NT))


def left_terms(tokens_ref, acts_ref, base_ref, out_ref):
    z = tokens_ref[0]
    for j in range(1, tokens_ref.shape[0]):
        z = z + tokens_ref[j]
    z3 = stacked(z)
    half = out_ref.shape[1]
    for b in range(0, out_ref.shape[2], COLUMN_BLOCK):
        block = pl.ds(b, COLUMN_BLOCK)
        left = folded(dot(z3, acts_ref[:, block], NN)) + base_ref[:, block]
        out_ref[0, :, block] = left[:half]
        out_ref[1, :, block] = left[half:]


def cut_left(halves_ref, out_ref):
    chunks, rows, width = out_ref.shape
    groups = halves_ref.shape[1] // rows
    per = chunks // groups
    for i in range(per):
        block = pl.ds(i * width, width)
        total = halves_ref[0, :, block] + halves_ref[1, :, block]
        for g in range(groups):
            out_ref[g * per + i] = total[g * rows : (g + 1) * rows]


def sum_and_fan(in_ref, out_ref):
    total = in_ref[0]
    for j in range(1, in_ref.shape[0]):
        total = total + in_ref[j]
    for j in range(out_ref.shape[0]):
        out_ref[j] = total


def inverse_factor(gram, n):
    row_at = lax.broadcasted_iota(jnp.int32, (n, 2 * n), 0)
    col_at = lax.broadcasted_iota(jnp.int32, (n, 2 * n), 1)
    unit = (col_at == row_at + n).astype(F32)
    work = jnp.concatenate([gram, unit[:, n:]], axis=1)
    scale = jnp.zeros((n, 1), F32)
    rows_only = row_at[:, :1]
    for k in range(n):
        pivot = work[k : k + 1, k : k + 1]
        scale = jnp.where(rows_only == k, pivot, scale)
        if k < n - 1:
            factor = work[:, k : k + 1] / pivot
            factor = jnp.where(rows_only > k, factor, 0.0)
            work = work - factor * work[k : k + 1, :]
    return work[:, n:] / jnp.sqrt(scale)


def joined(ref, groups, i):
    per = ref.shape[0] // groups
    return jnp.concatenate([ref[g * per + i] for g in range(groups)], axis=0)


def token_products(left_ref, own_ref, sibling_ref, tokens_ref):
    chunks, rows, width = left_ref.shape
    half = tokens_ref.shape[1] // 2
    groups = half // rows
    own = jnp.zeros((3 * half, own_ref.shape[0]), F32)
    sibling = own
    for i in range(chunks // groups):
        block = pl.ds(i * width, width)
        l3 = stacked(joined(left_ref, groups, i))
        own = own + dot(l3, own_ref[:, block], NT)
        sibling = sibling + dot(l3, sibling_ref[:, block], NT)
    both = jnp.concatenate([folded(own), folded(sibling)], axis=0)
    for j in range(tokens_ref.shape[0]):
        tokens_ref[j] = both


def residual_right(left_ref, own_ref, sibling_ref, out_ref):
    chunks, rows, width = left_ref.shape
    half = out_ref.shape[0]
    groups = half // rows
    total = jnp.zeros((3 * half, out_ref.shape[1]), F32)
    for i in range(chunks // groups):
        block = pl.ds(i * width, width)
        l3 = stacked(joined(left_ref, groups, i))
        total = total + dot(l3, own_ref[block, :], NN) + dot(l3, sibling_ref[block, :], NN)
    out_ref[...] = folded(total)


def orthonormal(core_ref, at_ref, own_ref, other_ref, basis3_ref, factor_ref, inverse_ref, left3, basis):
    n, width = basis.shape
    step = own_ref.shape[2]
    groups = n // (2 * own_ref.shape[1])
    first = core_ref[0] == 0
    nine = jnp.zeros((3 * n, 3 * n), F32)
    for i in range(width // step):
        block = pl.ds(i * step, step)
        mine, theirs = joined(own_ref, groups, i), joined(other_ref, groups, i)
        l3 = stacked(jnp.concatenate([jnp.where(first, mine, theirs), jnp.where(first, theirs, mine)], axis=0))
        left3[:, block] = l3
        nine = nine + dot(l3, l3, NT)
    part = lambda i, j: nine[i * n : (i + 1) * n, j * n : (j + 1) * n]
    gram = part(0, 0) + (
        (part(0, 1) + part(1, 0)) + ((part(0, 2) + part(2, 0) + part(1, 1)) + ((part(1, 2) + part(2, 1)) + part(2, 2)))
    )
    inverse = inverse_factor(gram, n)
    inverse_ref[...] = inverse
    wide = six_left(inverse)
    for b in range(0, width, COLUMN_BLOCK):
        block = pl.ds(b, COLUMN_BLOCK)
        l3 = left3[:, block]
        part_of = dot(wide, jnp.concatenate([l3, l3[: 2 * n], l3[:n]], axis=0), NN)
        basis[:, block] = part_of
        basis3_ref[:, block] = stacked(part_of)
    columns = factor_ref.shape[1]
    own = pl.ds(pl.multiple_of(at_ref[0] * columns, 128), columns)
    factor_ref[...] = basis[:, own] * jnp.sqrt(F32(width))


def right_terms(tokens_ref, base_ref, own_ref, sibling_ref, out_ref):
    total = base_ref[...]
    half = total.shape[0]
    blocks, _, tokens = tokens_ref.shape
    for j in range(blocks):
        here = pl.ds(j * tokens, tokens)
        total = total + folded(
            dot(stacked(tokens_ref[j, :half]), own_ref[here, :], NN)
            + dot(stacked(tokens_ref[j, half:]), sibling_ref[here, :], NN)
        )
    for j in range(out_ref.shape[0]):
        out_ref[j] = total


def sum_right(in_ref, out_ref):
    total = in_ref[0]
    for j in range(1, in_ref.shape[0]):
        total = total + in_ref[j]
    out_ref[...] = total


def right_and_base(core_ref, scale_ref, own_ref, other_ref, inverse_ref, basis3_ref, residual_ref, right_ref, out_ref):
    first = core_ref[0] == 0
    own, other = own_ref[...], other_ref[...]
    raw = jnp.concatenate([jnp.where(first, own, other), jnp.where(first, other, own)], axis=0)
    right = dot(six_left(inverse_ref[...]), six_right(raw), NN) * scale_ref[0]
    right_ref[...] = right
    high, middle, low = pieces(right)
    right_t = jnp.concatenate([high, high, high, middle, middle, low], axis=0).T
    n = right.shape[0]
    for b in range(0, out_ref.shape[0], COLUMN_BLOCK):
        block = pl.ds(b, COLUMN_BLOCK)
        b3 = basis3_ref[:, block]
        product = dot(right_t, jnp.concatenate([b3, b3[: 2 * n], b3[:n]], axis=0), NN)
        out_ref[block, :] = residual_ref[block, :].astype(F32) - product.T


def residual_terms(grads_ref, acts_ref, base_ref, out_ref, grads_t):
    @pl.when(pl.program_id(0) == 0)
    def _():
        grads_t[...] = grads_ref[...].T

    gradient_t = dot(grads_t[...], acts_ref[...], NN)
    out_ref[...] = (gradient_t.T + base_ref[...]).astype(BF16)


def shards(activations, out_grads, residual, q_start):
    acts, grads, resid = activations[0], out_grads[0], residual[0]
    own_tokens, width = acts.shape
    all_tokens, columns = grads.shape
    rank = q_start.shape[1]
    nt, nxz = lax.axis_size("tensor"), lax.axis_size(XZ)
    replicas = lax.axis_size(("x", "z", "core"))
    half = rank // 2
    chunk = (nxz, 4, half * width // (4 * nxz))
    core = lax.axis_index("core").astype(jnp.int32).reshape(1)
    swap = [(0, 1), (1, 0)]
    qt = q_start.T

    with jax.named_scope("gather_activations"):
        gathered = lax.all_gather(acts, "tensor", axis=0, tiled=True)

    with jax.named_scope("token_terms"):
        z = call(token_terms, ((nt, rank, own_tokens), F32), 2 * 3 * rank * columns * all_tokens, 2**19)(qt, grads)
        z = lax.all_to_all(z, "tensor", 0, 0)
    with jax.named_scope("residual_left"):
        base = call(residual_left, ((rank, width), F32), 2 * 3 * rank * columns * width, 2**22)(qt, resid)
    with jax.named_scope("sibling"):
        base, *mine = lax.optimization_barrier((base, resid, acts, grads))
        resid_sib, acts_sib, grads_sib = [lax.ppermute(x, "core", swap) for x in mine]
    with jax.named_scope("left_terms"):
        left = call(left_terms, ((2, half, width), F32), 2 * 3 * rank * own_tokens * width, 2**22)(z, acts, base)
    with jax.named_scope("left_sum"):
        left = lax.all_to_all(left, "core", 0, 0)
        left = call(cut_left, (chunk, F32), 2**18, 2**20)(left)
        left = lax.all_to_all(left, XZ, 0, 0)
        left = call(sum_and_fan, ((nt,) + chunk[1:], F32), 2**18, 2**19)(left)
        left = lax.all_to_all(left, "tensor", 0, 0)
        left = call(sum_and_fan, (chunk, F32), 2**18, 2**19)(left)
        left_own = lax.all_to_all(left, XZ, 0, 0)
    with jax.named_scope("token_products"):
        tokens = call(
            token_products, ((nt, rank, own_tokens), F32), 2 * 3 * rank * own_tokens * width, 2**22
        )(left_own, acts, acts_sib)
        tokens = lax.all_to_all(tokens, "tensor", 0, 0)
    with jax.named_scope("residual_right"):
        base = call(residual_right, ((half, columns), F32), 2 * 3 * rank * columns * width, 2**22)(
            left_own, resid, resid_sib
        )
    with jax.named_scope("orthonormal"):
        left_other = lax.ppermute(left_own, "core", swap)
    with jax.named_scope("right_terms"):
        right = call(right_terms, ((nxz, half, columns), F32), 2 * 3 * rank * all_tokens * columns, 2**19)(
            tokens, base, grads, grads_sib
        )
    with jax.named_scope("right_sum"):
        right = lax.all_to_all(right, XZ, 0, 0)
    with jax.named_scope("orthonormal"):
        at = lax.axis_index("tensor").astype(jnp.int32).reshape(1)
        basis3, p_factor, inverse = call(
            orthonormal,
            [((3 * rank, width), BF16), ((rank, width // nt), F32), ((rank, rank), F32)],
            2**32,
            2**22,
        )(
            core,
            at,
            left_own,
            left_other,
            scratch=(pltpu.VMEM((3 * rank, width), BF16), pltpu.VMEM((rank, width), F32)),
            smem=(0, 1),
        )
    with jax.named_scope("right_sum"):
        right, basis3 = lax.optimization_barrier((right, basis3))
        own = call(sum_right, ((half, columns), F32), 2**16, 2**18)(right)
        other = lax.ppermute(own, "core", swap)
    with jax.named_scope("right_and_base"):
        right, base = call(
            right_and_base, [((rank, columns), F32), ((width, columns), F32)], 2 * 6 * rank * width * columns, 2**22
        )(core, jnp.full((1,), 1.0 / replicas, F32), own, other, inverse, basis3, resid, smem=(0, 1))
    with jax.named_scope("residual_out"):
        residual_out = pl.pallas_call(
            residual_terms,
            grid=(width // ROW_BLOCK,),
            out_shape=jax.ShapeDtypeStruct((width, columns), BF16),
            in_specs=[
                pl.BlockSpec((all_tokens, columns), lambda i: (0, 0)),
                pl.BlockSpec((all_tokens, ROW_BLOCK), lambda i: (0, i)),
                pl.BlockSpec((ROW_BLOCK, columns), lambda i: (i, 0)),
            ],
            out_specs=pl.BlockSpec((ROW_BLOCK, columns), lambda i: (i, 0)),
            scratch_shapes=[pltpu.VMEM((columns, all_tokens), BF16)],
            compiler_params=pltpu.CompilerParams(vmem_limit_bytes=54 * 1024 * 1024),
            cost_estimate=pl.CostEstimate(flops=2**31, bytes_accessed=2**24, transcendentals=0),
        )(grads, gathered, base)
    return (p_factor.T, right.T, residual_out[None])


def solution(mesh):
    replicas, tensor = mesh.devices.shape
    zs = 8
    fine = Mesh(mesh.devices.reshape(replicas // (2 * zs), zs, 2, tensor), ("x", "z", "core", "tensor"))
    dp = ("x", "z", "core")
    return jax.shard_map(
        shards,
        mesh=fine,
        in_specs=(
            P(dp, "tensor", None),
            P(dp, None, "tensor"),
            P(dp, None, "tensor"),
            P("tensor", None),
        ),
        out_specs=(P("tensor", None), P("tensor", None), P(dp, None, "tensor")),
        check_vma=False,
    )
```

time: 159 us -> 151 us (0.950)
  blocking collectives: 64.4 us -> 18.7 us
  starting transfers between devices: 28.4 us -> 58 us
  Pallas kernels: 12.5 us -> 23.9 us
  waiting for transfers between devices: 23.9 us -> 31.5 us
  matrix products: 5.8 us -> 0 us
  local copies, waits for them, and re-layouts: 6.99 us -> 3.47 us
    all_to_all x3 -> x0, blocking collectives: 45.8 us -> none  [the longest x1 22.9 us: shards(): left = lax.all_to_all(left, XZ, 0, 0)]
    all_to_all x1 -> x3, starting transfers between devices: 4.92 us -> 24.7 us  [the longest x1 10.7 us: shards(): left = lax.all_to_all(left, XZ, 0, 0)]
    ppermute x0 -> x4, starting transfers between devices: none -> 14.9 us  [the longest x3 8.54 us: shards(): lax.ppermute(x, 'core', swap)]
    all_to_all x1 -> x3, waiting for transfers between devices: 8.14 us -> 15.1 us  [the longest x1 5.96 us: shards(): left = lax.all_to_all(left, XZ, 0, 0)]
    pallas_call x0 -> x1, Pallas kernels: none -> 6.62 us  [shards(): pl.pallas_call(residual_terms, grid=(width // ROW_BLOCK,), out_shape=jax....]
    all_gather x1, waiting for transfers between devices: 0.02 us -> 6.41 us  [shards(): gathered = lax.all_gather(acts, 'tensor', axis=0, tiled=True)]
    all_to_all x1, waiting for transfers between devices: 6.93 us -> 0.96 us  [shards(): tokens = lax.all_to_all(tokens, 'tensor', 0, 0)]
    dot_general x1 -> x0, matrix products: 5.8 us -> none  [shards(): lax.dot_general(gathered, grads, (((0,), (0,)), ((), ())), preferred_elem...]
  transfers between devices with their start and end apart: 6 -> 11, of which waited for: 4 -> 7; matrix products, arithmetic and copies ran while one was open for 5% -> 0% of each run, Pallas kernels for 7% -> 12%
where the time goes in v2:
time: 151 us; the launch traced here: 150 us
  starting transfers between devices  58 us (38%)
  waiting for transfers between devices  31.5 us (21%)
  Pallas kernels  23.9 us (16%)
  blocking collectives  18.7 us (12%)
  between operations  14.2 us (9%)
  local copies, waits for them, and re-layouts  3.47 us (2%)
    pallas_call x12, Pallas kernels, run(): pl.pallas_call(kernel, out_shape=shapes if several else shapes[0], in_spe...  17.3 us
    all_to_all x1, starting transfers between devices, shards(): left = lax.all_to_all(left, XZ, 0, 0)  10.7 us
    all_to_all x1, blocking collectives, shards(): left = lax.all_to_all(left, 'tensor', 0, 0)  10.6 us
    ppermute x3, starting transfers between devices, shards(): lax.ppermute(x, 'core', swap)  8.54 us
    all_to_all x1, blocking collectives, shards(): left = lax.all_to_all(left, 'core', 0, 0)  8.04 us
    all_to_all x1, starting transfers between devices, shards(): left_own = lax.all_to_all(left, XZ, 0, 0)  7.83 us
    all_to_all x1, starting transfers between devices, shards(): z = lax.all_to_all(z, 'tensor', 0, 0)  7.65 us
    all_to_all x1, waiting for transfers between devices, shards(): z = lax.all_to_all(z, 'tensor', 0, 0)  7.55 us
  transfers between devices with their start and end apart: 11, of which 7 were waited for; matrix products, arithmetic and copies ran while one was open for 0% of the time, Pallas kernels for 12%

profile of v2, /device:TPU:1, one launch (start us, length us, event | category | flops | bytes accessed | tf_op | source)
XLA Modules:
  0.0 149.8 jit_solution(7740446272297993313)
XLA Ops:
  8.1 0.9 token_terms.1
  9.1 7.7 %all-to-all-start = ((f32[8,32,128]{2,1,0:T(8,128)}), f32[8,32,128]{2,1,0:T(8,128)}, u32[]{:S(2)}, u32[]{:S(2)}) async-start(f32[8,32,128]{2,1,0:T(8,128)} %token_terms.1), calls=%async_computation | async-start | bytes 262144 | tf_op jit(solution)/shard_map/token_terms/all_to_all | solution.py:259
  17.3 7.6 %all-to-all-done.tokens_ref = f32[8,32,128]{2,1,0:T(8,128)} async-done(((f32[8,32,128]{2,1,0:T(8,128)}), f32[8,32,128]{2,1,0:T(8,128)}, u32[]{:S(2)}, u32[]{:S(2)}) %all-to-all-start) | async-done | bytes 131104 | tf_op jit(solution)/shard_map/token_terms/all_to_all | solution.py:259
  24.9 1.3 left_terms.1
  26.2 8.0 %all_to_all.35.halves_ref = f32[2,16,5120]{2,1,0:T(8,128)S(1)} all-to-all(f32[2,16,5120]{2,1,0:T(8,128)S(1)} %left_terms.1), channel_id=1, replica_groups=mesh['x'=4,'z'=8,'core'=2,'tensor'=8] {'core'}, dimensions={0} | all-to-all | bytes 1310720 | tf_op jit(solution)/shard_map/left_sum/all_to_all | solution.py:268
  34.2 0.8 left_sum.3
  35.0 10.7 %all-to-all-start.2 = ((f32[32,4,640]{2,1,0:T(4,128)}), f32[32,4,640]{2,1,0:T(4,128)S(1)}, u32[]{:S(2)}, u32[]{:S(2)}) async-start(f32[32,4,640]{2,1,0:T(4,128)} %left_sum.3), calls=%async_computation.2 | async-start | bytes 655360 | tf_op jit(solution)/shard_map/left_sum/all_to_all | solution.py:270
  45.8 2.6 %collective-permute-start.1 = (bf16[128,5120]{1,0:T(8,128)(2,1)S(1)}, bf16[128,5120]{1,0:T(8,128)(2,1)}, u32[]{:S(2)}, u32[]{:S(2)}) collective-permute-start(bf16[128,5120]{1,0:T(8,128)(2,1)S(1)} %bitcast.11), channel_id=1, source_target_pairs={{0,8},{8,0},{1,9},{9,1},{2,10},{10,2},{3,11},{11,3},{4,12},{12,4},... | collective-permute-start | bytes 3932168 | tf_op jit(solution)/shard_map/sibling/ppermute | solution.py:264
  48.3 1.9 %collective-permute-start.2 = (bf16[5120,128]{1,0:T(8,128)(2,1)S(1)}, bf16[5120,128]{1,0:T(8,128)(2,1)}, u32[]{:S(2)}, u32[]{:S(2)}) collective-permute-start(bf16[5120,128]{1,0:T(8,128)(2,1)S(1)} %bitcast.14), channel_id=1, source_target_pairs={{0,8},{8,0},{1,9},{9,1},{2,10},{10,2},{3,11},{11,3},{4,12},{12,4},... | collective-permute-start | bytes 3932168 | tf_op jit(solution)/shard_map/sibling/ppermute | solution.py:264
  50.3 6.0 %all-to-all-done.2.in_ref = f32[32,4,640]{2,1,0:T(4,128)S(1)} async-done(((f32[32,4,640]{2,1,0:T(4,128)}), f32[32,4,640]{2,1,0:T(4,128)S(1)}, u32[]{:S(2)}, u32[]{:S(2)}) %all-to-all-start.2) | async-done | bytes 327712 | tf_op jit(solution)/shard_map/left_sum/all_to_all | solution.py:270
  56.3 10.6 %all_to_all.36.in_ref = f32[8,4,640]{2,1,0:T(4,128)S(1)} all-to-all(f32[8,4,640]{2,1,0:T(4,128)S(1)} %left_sum.4), channel_id=1, replica_groups=mesh['x'=4,'z'=8,'core'=2,'tensor'=8] {'tensor'}, dimensions={0} | all-to-all | bytes 163840 | tf_op jit(solution)/shard_map/left_sum/all_to_all | solution.py:272
  66.9 0.8 left_sum.5
  67.7 7.8 %all-to-all-start.4 = ((f32[32,4,640]{2,1,0:T(4,128)}), f32[32,4,640]{2,1,0:T(4,128)S(1)}, u32[]{:S(2)}, u32[]{:S(2)}) async-start(f32[32,4,640]{2,1,0:T(4,128)} %left_sum.5), calls=%async_computation.4 | async-start | bytes 655360 | tf_op jit(solution)/shard_map/left_sum/all_to_all | solution.py:274
  75.5 4.1 %collective-permute-start.3 = (bf16[1024,128]{1,0:T(8,128)(2,1)S(1)}, bf16[1024,128]{1,0:T(8,128)(2,1)}, u32[]{:S(2)}, u32[]{:S(2)}) collective-permute-start(bf16[1024,128]{1,0:T(8,128)(2,1)S(1)} %bitcast.19), channel_id=1, source_target_pairs={{0,8},{8,0},{1,9},{9,1},{2,10},{10,2},{3,11},{11,3},{4,12},{12,4},... | collective-permute-start | bytes 786440 | tf_op jit(solution)/shard_map/sibling/ppermute | solution.py:264
  79.6 5.9 %all-to-all-done.4.own_ref.left_ref = f32[32,4,640]{2,1,0:T(4,128)S(1)} async-done(((f32[32,4,640]{2,1,0:T(4,128)}), f32[32,4,640]{2,1,0:T(4,128)S(1)}, u32[]{:S(2)}, u32[]{:S(2)}) %all-to-all-start.4) | async-done | bytes 327712 | tf_op jit(solution)/shard_map/left_sum/all_to_all | solution.py:274
  85.5 3.1 %token_products.1 = f32[8,32,128]{2,1,0:T(8,128)} custom-call(f32[32,4,640]{2,1,0:T(4,128)S(1)} %all-to-all-done.4.own_ref.left_ref, bf16[128,5120]{1,0:T(8,128)(2,1)S(1)} %bitcast.12, bf16[128,5120]{1,0:T(8,128)(2,1)} %collective-permute-done.1.sibling_ref), custom_call_target="tpu_custom_call" | custom-call | flops 125829120 | bytes 4194304 | tf_op jit(solution)/shard_map/token_products/pallas_call | solution.py:25
  88.6 3.4 %all-to-all-start.5 = ((f32[8,32,128]{2,1,0:T(8,128)}), f32[8,32,128]{2,1,0:T(8,128)S(1)}, u32[]{:S(2)}, u32[]{:S(2)}) async-start(f32[8,32,128]{2,1,0:T(8,128)} %token_products.1), calls=%async_computation.5 | async-start | bytes 262144 | tf_op jit(solution)/shard_map/token_products/all_to_all | solution.py:279
  92.0 6.3 %collective-permute-start = (f32[32,4,640]{2,1,0:T(4,128)S(1)}, f32[32,4,640]{2,1,0:T(4,128)S(1)}, u32[]{:S(2)}, u32[]{:S(2)}) collective-permute-start(f32[32,4,640]{2,1,0:T(4,128)S(1)} %all-to-all-done.4.own_ref.left_ref), channel_id=1, source_target_pairs={{0,8},{8,0},{1,9},{9,1},{2,10},{10,2},{3,11},{11,3},{4,12},{12,4},... | collective-permute-start | bytes 983048 | tf_op jit(solution)/shard_map/orthonormal/ppermute | solution.py:285
  98.3 1.9 %residual_right.1.base_ref = f32[16,128]{1,0:T(8,128)S(1)} custom-call(f32[32,4,640]{2,1,0:T(4,128)S(1)} %all-to-all-done.4.own_ref.left_ref, bf16[5120,128]{1,0:T(8,128)(2,1)S(1)} %bitcast.15, bf16[5120,128]{1,0:T(8,128)(2,1)} %collective-permute-done.2.sibling_ref), custom_call_target="tpu_custom_call" | custom-call | flops 125829120 | bytes 4194304 | tf_op jit(solution)/shard_map/residual_right/pallas_call | solution.py:25
  100.2 1.0 all-to-all-done.5.tokens_ref
  101.2 2.0 %right_terms.1 = f32[32,16,128]{2,1,0:T(8,128)} custom-call(f32[8,32,128]{2,1,0:T(8,128)S(1)} %all-to-all-done.5.tokens_ref, f32[16,128]{1,0:T(8,128)S(1)} %residual_right.1.base_ref, bf16[1024,128]{1,0:T(8,128)(2,1)S(1)} %bitcast.20, bf16[1024,128]{1,0:T(8,128)(2,1)} %collective-permute-done.3.sibling_ref), custom_call_target="tpu_custom_call" | custom-call | flops 25165824 | bytes 524288 | tf_op jit(solution)/shard_map/right_terms/pallas_call | solution.py:25
  103.2 6.1 %all-to-all-start.6 = ((f32[32,16,128]{2,1,0:T(8,128)}), f32[32,16,128]{2,1,0:T(8,128)S(1)}, u32[]{:S(2)}, u32[]{:S(2)}) async-start(f32[32,16,128]{2,1,0:T(8,128)} %right_terms.1), calls=%async_computation.6 | async-start | bytes 524288 | tf_op jit(solution)/shard_map/right_sum/all_to_all | solution.py:291
  109.3 0.7 copy-done.5
  110.0 1.0 copy-done.6
  111.0 4.7 %orthonormal.1 = (bf16[96,5120]{1,0:T(8,128)(2,1)S(1)}, f32[32,640]{1,0:T(8,128)}, f32[32,32]{1,0:T(8,128)S(1)}) custom-call(s32[1]{0:T(128)} %bitcast.core_ref, s32[1]{0:T(128)} %bitcast.1.at_ref, f32[32,4,640]{2,1,0:T(4,128)S(1)} %all-to-all-done.4.own_ref.left_ref, f32[32,4,640]{2,1,0:T(4,128)S(1)} %copy-done.6), custom_call_target="tpu_custom_call" | custom-call | flops 4294967296 | bytes 4194304 | tf_op jit(solution)/shard_map/orthonormal/pallas_call | solution.py:25
  115.7 3.2 %all-to-all-done.6.in_ref = f32[32,16,128]{2,1,0:T(8,128)S(1)} async-done(((f32[32,16,128]{2,1,0:T(8,128)}), f32[32,16,128]{2,1,0:T(8,128)S(1)}, u32[]{:S(2)}, u32[]{:S(2)}) %all-to-all-start.6) | async-done | bytes 262176 | tf_op jit(solution)/shard_map/right_sum/all_to_all | solution.py:291
  119.0 7.4 %collective-permute-start.4 = (f32[16,128]{1,0:T(8,128)S(1)}, f32[16,128]{1,0:T(8,128)S(1)}, u32[]{:S(2)}, u32[]{:S(2)}) collective-permute-start(f32[16,128]{1,0:T(8,128)S(1)} %right_sum.1.own_ref), channel_id=1, source_target_pairs={{0,8},{8,0},{1,9},{9,1},{2,10},{10,2},{3,11},{11,3},{4,12},{12,4},... | collective-permute-start | bytes 24584 | tf_op jit(solution)/shard_map/right_sum/ppermute | solution.py:310
  126.4 0.8 collective-permute-done.4.other_ref
  127.2 1.1 right_and_base.1
  128.3 1.6 %copy-done.2 = f32[5120,128]{1,0:T(8,128)} copy-done((f32[5120,128]{1,0:T(8,128)}, f32[5120,128]{1,0:T(8,128)S(1)}, u32[]{:S(2)}) %copy-start.2) | copy-done | bytes 2621464
  129.9 6.4 %all-gather.3.cloned.1.call-done = bf16[1,1024,5120]{2,1,0:T(8,128)(2,1)} async-done(((bf16[1,128,5120]{2,1,0:T(8,128)(2,1)}), bf16[1,1024,5120]{2,1,0:T(8,128)(2,1)}) %all-gather.3.cloned.1.call-update) | async-done | bytes 10485776 | tf_op jit(solution)/shard_map/gather_activations/all_gather | solution.py:255
  136.3 6.6 %residual_out.1 = bf16[5120,128]{1,0:T(8,128)(2,1)} custom-call(bf16[1024,128]{1,0:T(8,128)(2,1)} %bitcast.17, bf16[1024,5120]{1,0:T(8,128)(2,1)} %bitcast.23, f32[5120,128]{1,0:T(8,128)} %copy-done.2), custom_call_target="tpu_custom_call" | custom-call | flops 2147483648 | bytes 16777216 | tf_op jit(solution)/shard_map/residual_out/pallas_call | solution.py:316
  (20 shorter events, 1.6 us)
Async XLA Ops:
  7.2 0.8 copy-start.4
  7.2 1.0 copy-start.3
  7.2 9.5 %copy-start.1 = (bf16[1,5120,128]{2,1,0:T(8,128)(2,1)S(1)}, bf16[1,5120,128]{2,1,0:T(8,128)(2,1)}, u32[]{:S(2)}) copy-start(bf16[1,5120,128]{2,1,0:T(8,128)(2,1)} %param.6) | copy-start | bytes 3932164
  7.2 129.1 %all-gather.3.cloned.1.call-start = ((), (), s32[]{:S(2)}) async-start(), calls=%async_computation.7 | async-start | bytes 11796480 | tf_op jit(solution)/shard_map/gather_activations/all_gather | solution.py:255
  8.1 16.7 %copy-start = (bf16[1,128,5120]{2,1,0:T(8,128)(2,1)S(1)}, bf16[1,128,5120]{2,1,0:T(8,128)(2,1)}, u32[]{:S(2)}) copy-start(bf16[1,128,5120]{2,1,0:T(8,128)(2,1)} %param.4) | copy-start | bytes 3932164
  9.1 15.8 %all-to-all-start = ((f32[8,32,128]{2,1,0:T(8,128)}), f32[8,32,128]{2,1,0:T(8,128)}, u32[]{:S(2)}, u32[]{:S(2)}) async-start(f32[8,32,128]{2,1,0:T(8,128)} %token_terms.1), calls=%async_computation | async-start | bytes 262144 | tf_op jit(solution)/shard_map/token_terms/all_to_all | solution.py:259
  35.0 21.2 %all-to-all-start.2 = ((f32[32,4,640]{2,1,0:T(4,128)}), f32[32,4,640]{2,1,0:T(4,128)S(1)}, u32[]{:S(2)}, u32[]{:S(2)}) async-start(f32[32,4,640]{2,1,0:T(4,128)} %left_sum.3), calls=%async_computation.2 | async-start | bytes 655360 | tf_op jit(solution)/shard_map/left_sum/all_to_all | solution.py:270
  45.8 33.8 %collective-permute-start.1 = (bf16[128,5120]{1,0:T(8,128)(2,1)S(1)}, bf16[128,5120]{1,0:T(8,128)(2,1)}, u32[]{:S(2)}, u32[]{:S(2)}) collective-permute-start(bf16[128,5120]{1,0:T(8,128)(2,1)S(1)} %bitcast.11), channel_id=1, source_target_pairs={{0,8},{8,0},{1,9},{9,1},{2,10},{10,2},{3,11},{11,3},{4,12},{12,4},... | collective-permute-start | bytes 3932168 | tf_op jit(solution)/shard_map/sibling/ppermute | solution.py:264
  48.3 50.0 %collective-permute-start.2 = (bf16[5120,128]{1,0:T(8,128)(2,1)S(1)}, bf16[5120,128]{1,0:T(8,128)(2,1)}, u32[]{:S(2)}, u32[]{:S(2)}) collective-permute-start(bf16[5120,128]{1,0:T(8,128)(2,1)S(1)} %bitcast.14), channel_id=1, source_target_pairs={{0,8},{8,0},{1,9},{9,1},{2,10},{10,2},{3,11},{11,3},{4,12},{12,4},... | collective-permute-start | bytes 3932168 | tf_op jit(solution)/shard_map/sibling/ppermute | solution.py:264
  67.7 17.8 %all-to-all-start.4 = ((f32[32,4,640]{2,1,0:T(4,128)}), f32[32,4,640]{2,1,0:T(4,128)S(1)}, u32[]{:S(2)}, u32[]{:S(2)}) async-start(f32[32,4,640]{2,1,0:T(4,128)} %left_sum.5), calls=%async_computation.4 | async-start | bytes 655360 | tf_op jit(solution)/shard_map/left_sum/all_to_all | solution.py:274
  75.5 24.8 %collective-permute-start.3 = (bf16[1024,128]{1,0:T(8,128)(2,1)S(1)}, bf16[1024,128]{1,0:T(8,128)(2,1)}, u32[]{:S(2)}, u32[]{:S(2)}) collective-permute-start(bf16[1024,128]{1,0:T(8,128)(2,1)S(1)} %bitcast.19), channel_id=1, source_target_pairs={{0,8},{8,0},{1,9},{9,1},{2,10},{10,2},{3,11},{11,3},{4,12},{12,4},... | collective-permute-start | bytes 786440 | tf_op jit(solution)/shard_map/sibling/ppermute | solution.py:264
  88.6 12.6 %all-to-all-start.5 = ((f32[8,32,128]{2,1,0:T(8,128)}), f32[8,32,128]{2,1,0:T(8,128)S(1)}, u32[]{:S(2)}, u32[]{:S(2)}) async-start(f32[8,32,128]{2,1,0:T(8,128)} %token_products.1), calls=%async_computation.5 | async-start | bytes 262144 | tf_op jit(solution)/shard_map/token_products/all_to_all | solution.py:279
  92.0 17.3 %collective-permute-start = (f32[32,4,640]{2,1,0:T(4,128)S(1)}, f32[32,4,640]{2,1,0:T(4,128)S(1)}, u32[]{:S(2)}, u32[]{:S(2)}) collective-permute-start(f32[32,4,640]{2,1,0:T(4,128)S(1)} %all-to-all-done.4.own_ref.left_ref), channel_id=1, source_target_pairs={{0,8},{8,0},{1,9},{9,1},{2,10},{10,2},{3,11},{11,3},{4,12},{12,4},... | collective-permute-start | bytes 983048 | tf_op jit(solution)/shard_map/orthonormal/ppermute | solution.py:285
  103.2 15.7 %all-to-all-start.6 = ((f32[32,16,128]{2,1,0:T(8,128)}), f32[32,16,128]{2,1,0:T(8,128)S(1)}, u32[]{:S(2)}, u32[]{:S(2)}) async-start(f32[32,16,128]{2,1,0:T(8,128)} %right_terms.1), calls=%async_computation.6 | async-start | bytes 524288 | tf_op jit(solution)/shard_map/right_sum/all_to_all | solution.py:291
  109.3 0.7 copy-start.5
  110.0 1.0 copy-start.6
  119.0 8.2 %collective-permute-start.4 = (f32[16,128]{1,0:T(8,128)S(1)}, f32[16,128]{1,0:T(8,128)S(1)}, u32[]{:S(2)}, u32[]{:S(2)}) collective-permute-start(f32[16,128]{1,0:T(8,128)S(1)} %right_sum.1.own_ref), channel_id=1, source_target_pairs={{0,8},{8,0},{1,9},{9,1},{2,10},{10,2},{3,11},{11,3},{4,12},{12,4},... | collective-permute-start | bytes 24584 | tf_op jit(solution)/shard_map/right_sum/ppermute | solution.py:310
  128.3 1.6 %copy-start.2 = (f32[5120,128]{1,0:T(8,128)}, f32[5120,128]{1,0:T(8,128)S(1)}, u32[]{:S(2)}) copy-start(f32[5120,128]{1,0:T(8,128)S(1)} %get-tuple-element.24.base_ref) | copy-start | bytes 7864324
Sparse Core Ops, SparseCore 0:
  10.1 126.1 all-gather.2

commit v3 on v2

--- a/solution.py
+++ b/solution.py
@@ -13,7 +13,7 @@
 VMEM = pl.BlockSpec(memory_space=pltpu.VMEM)
 SMEM = pl.BlockSpec(memory_space=pltpu.SMEM)
 XZ = ("x", "z")
-COLUMN_BLOCK = 640
+COLUMN_BLOCK = 1280
 ROW_BLOCK = 2560
 
 
@@ -213,7 +213,11 @@
     out_ref[...] = total
 
 
-def right_and_base(core_ref, scale_ref, own_ref, other_ref, inverse_ref, basis3_ref, residual_ref, right_ref, out_ref):
+def right_and_base(
+    core_ref, scale_ref, own_ref, other_ref, inverse_ref, basis3_ref, residual_ref, grads_ref,
+    right_ref, out_ref, grads_t_ref,
+):
+    grads_t_ref[...] = grads_ref[...].T
     first = core_ref[0] == 0
     own, other = own_ref[...], other_ref[...]
     raw = jnp.concatenate([jnp.where(first, own, other), jnp.where(first, other, own)], axis=0)
@@ -229,12 +233,8 @@
         out_ref[block, :] = residual_ref[block, :].astype(F32) - product.T
 
 
-def residual_terms(grads_ref, acts_ref, base_ref, out_ref, grads_t):
-    @pl.when(pl.program_id(0) == 0)
-    def _():
-        grads_t[...] = grads_ref[...].T
-
-    gradient_t = dot(grads_t[...], acts_ref[...], NN)
+def residual_terms(grads_t_ref, acts_ref, base_ref, out_ref):
+    gradient_t = dot(grads_t_ref[...], acts_ref[...], NN)
     out_ref[...] = (gradient_t.T + base_ref[...]).astype(BF16)
 
 
@@ -309,24 +309,26 @@
         own = call(sum_right, ((half, columns), F32), 2**16, 2**18)(right)
         other = lax.ppermute(own, "core", swap)
     with jax.named_scope("right_and_base"):
-        right, base = call(
-            right_and_base, [((rank, columns), F32), ((width, columns), F32)], 2 * 6 * rank * width * columns, 2**22
-        )(core, jnp.full((1,), 1.0 / replicas, F32), own, other, inverse, basis3, resid, smem=(0, 1))
+        right, base, grads_t = call(
+            right_and_base,
+            [((rank, columns), F32), ((width, columns), F32), ((columns, all_tokens), BF16)],
+            2 * 6 * rank * width * columns,
+            2**22,
+        )(core, jnp.full((1,), 1.0 / replicas, F32), own, other, inverse, basis3, resid, grads, smem=(0, 1))
     with jax.named_scope("residual_out"):
         residual_out = pl.pallas_call(
             residual_terms,
             grid=(width // ROW_BLOCK,),
             out_shape=jax.ShapeDtypeStruct((width, columns), BF16),
             in_specs=[
-                pl.BlockSpec((all_tokens, columns), lambda i: (0, 0)),
+                pl.BlockSpec((columns, all_tokens), lambda i: (0, 0)),
                 pl.BlockSpec((all_tokens, ROW_BLOCK), lambda i: (0, i)),
                 pl.BlockSpec((ROW_BLOCK, columns), lambda i: (i, 0)),
             ],
             out_specs=pl.BlockSpec((ROW_BLOCK, columns), lambda i: (i, 0)),
-            scratch_shapes=[pltpu.VMEM((columns, all_tokens), BF16)],
             compiler_params=pltpu.CompilerParams(vmem_limit_bytes=54 * 1024 * 1024),
             cost_estimate=pl.CostEstimate(flops=2**31, bytes_accessed=2**24, transcendentals=0),
-        )(grads, gathered, base)
+        )(grads_t, gathered, base)
     return (p_factor.T, right.T, residual_out[None])
 
 

time: 151 us -> 151 us (level)
    all_to_all x1, waiting for transfers between devices: 3.25 us -> 5.03 us  [shards(): right = lax.all_to_all(right, XZ, 0, 0)]
    unnamed x14 -> x12, local copies, waits for them, and re-layouts: 3.47 us -> 2.48 us
  transfers between devices with their start and end apart: 11 -> 11, of which waited for: 7 -> 7; matrix products, arithmetic and copies ran while one was open for 0% -> 0% of each run, Pallas kernels for 12% -> 11%
where the time goes in v3:
time: 151 us; the launch traced here: 150 us
  starting transfers between devices  58 us (38%)
  waiting for transfers between devices  32.6 us (22%)
  Pallas kernels  23.8 us (16%)
  blocking collectives  18.7 us (12%)
  between operations  14.2 us (9%)
  local copies, waits for them, and re-layouts  2.48 us (2%)
    pallas_call x12, Pallas kernels, run(): pl.pallas_call(kernel, out_shape=shapes if several else shapes[0], in_spe...  17.2 us
    all_to_all x1, starting transfers between devices, shards(): left = lax.all_to_all(left, XZ, 0, 0)  10.8 us
    all_to_all x1, blocking collectives, shards(): left = lax.all_to_all(left, 'tensor', 0, 0)  10.6 us
    ppermute x3, starting transfers between devices, shards(): lax.ppermute(x, 'core', swap)  8.54 us
    all_to_all x1, blocking collectives, shards(): left = lax.all_to_all(left, 'core', 0, 0)  8.04 us
    all_to_all x1, starting transfers between devices, shards(): left_own = lax.all_to_all(left, XZ, 0, 0)  7.83 us
    all_to_all x1, starting transfers between devices, shards(): z = lax.all_to_all(z, 'tensor', 0, 0)  7.65 us
    all_to_all x1, waiting for transfers between devices, shards(): z = lax.all_to_all(z, 'tensor', 0, 0)  7.6 us
  transfers between devices with their start and end apart: 11, of which 7 were waited for; matrix products, arithmetic and copies ran while one was open for 0% of the time, Pallas kernels for 11%

profile of v3, /device:TPU:1, one launch (start us, length us, event | category | flops | bytes accessed | tf_op | source)
XLA Modules:
  0.0 149.8 jit_solution(17750219044456115057)
XLA Ops:
  7.2 0.7 all-gather.3.cloned.1.call-update
  8.1 0.9 token_terms.1
  9.1 7.6 %all-to-all-start = ((f32[8,32,128]{2,1,0:T(8,128)}), f32[8,32,128]{2,1,0:T(8,128)}, u32[]{:S(2)}, u32[]{:S(2)}) async-start(f32[8,32,128]{2,1,0:T(8,128)} %token_terms.1), calls=%async_computation | async-start | bytes 262144 | tf_op jit(solution)/shard_map/token_terms/all_to_all | solution.py:259
  17.3 7.6 %all-to-all-done.tokens_ref = f32[8,32,128]{2,1,0:T(8,128)} async-done(((f32[8,32,128]{2,1,0:T(8,128)}), f32[8,32,128]{2,1,0:T(8,128)}, u32[]{:S(2)}, u32[]{:S(2)}) %all-to-all-start) | async-done | bytes 131104 | tf_op jit(solution)/shard_map/token_terms/all_to_all | solution.py:259
  24.9 1.3 left_terms.1
  26.2 8.0 %all_to_all.35.halves_ref = f32[2,16,5120]{2,1,0:T(8,128)S(1)} all-to-all(f32[2,16,5120]{2,1,0:T(8,128)S(1)} %left_terms.1), channel_id=1, replica_groups=mesh['x'=4,'z'=8,'core'=2,'tensor'=8] {'core'}, dimensions={0} | all-to-all | bytes 1310720 | tf_op jit(solution)/shard_map/left_sum/all_to_all | solution.py:268
  34.2 0.8 left_sum.3
  35.0 10.8 %all-to-all-start.2 = ((f32[32,4,640]{2,1,0:T(4,128)}), f32[32,4,640]{2,1,0:T(4,128)S(1)}, u32[]{:S(2)}, u32[]{:S(2)}) async-start(f32[32,4,640]{2,1,0:T(4,128)} %left_sum.3), calls=%async_computation.2 | async-start | bytes 655360 | tf_op jit(solution)/shard_map/left_sum/all_to_all | solution.py:270
  45.7 2.6 %collective-permute-start.1 = (bf16[128,5120]{1,0:T(8,128)(2,1)S(1)}, bf16[128,5120]{1,0:T(8,128)(2,1)}, u32[]{:S(2)}, u32[]{:S(2)}) collective-permute-start(bf16[128,5120]{1,0:T(8,128)(2,1)S(1)} %bitcast.15), channel_id=1, source_target_pairs={{0,8},{8,0},{1,9},{9,1},{2,10},{10,2},{3,11},{11,3},{4,12},{12,4},... | collective-permute-start | bytes 3932168 | tf_op jit(solution)/shard_map/sibling/ppermute | solution.py:264
  48.3 1.9 %collective-permute-start.2 = (bf16[5120,128]{1,0:T(8,128)(2,1)S(1)}, bf16[5120,128]{1,0:T(8,128)(2,1)}, u32[]{:S(2)}, u32[]{:S(2)}) collective-permute-start(bf16[5120,128]{1,0:T(8,128)(2,1)S(1)} %bitcast.11), channel_id=1, source_target_pairs={{0,8},{8,0},{1,9},{9,1},{2,10},{10,2},{3,11},{11,3},{4,12},{12,4},... | collective-permute-start | bytes 3932168 | tf_op jit(solution)/shard_map/sibling/ppermute | solution.py:264
  50.2 6.0 %all-to-all-done.2.in_ref = f32[32,4,640]{2,1,0:T(4,128)S(1)} async-done(((f32[32,4,640]{2,1,0:T(4,128)}), f32[32,4,640]{2,1,0:T(4,128)S(1)}, u32[]{:S(2)}, u32[]{:S(2)}) %all-to-all-start.2) | async-done | bytes 327712 | tf_op jit(solution)/shard_map/left_sum/all_to_all | solution.py:270
  56.3 10.6 %all_to_all.36.in_ref = f32[8,4,640]{2,1,0:T(4,128)S(1)} all-to-all(f32[8,4,640]{2,1,0:T(4,128)S(1)} %left_sum.4), channel_id=1, replica_groups=mesh['x'=4,'z'=8,'core'=2,'tensor'=8] {'tensor'}, dimensions={0} | all-to-all | bytes 163840 | tf_op jit(solution)/shard_map/left_sum/all_to_all | solution.py:272
  66.9 0.8 left_sum.5
  67.6 7.8 %all-to-all-start.4 = ((f32[32,4,640]{2,1,0:T(4,128)}), f32[32,4,640]{2,1,0:T(4,128)S(1)}, u32[]{:S(2)}, u32[]{:S(2)}) async-start(f32[32,4,640]{2,1,0:T(4,128)} %left_sum.5), calls=%async_computation.4 | async-start | bytes 655360 | tf_op jit(solution)/shard_map/left_sum/all_to_all | solution.py:274
  75.5 4.1 %collective-permute-start.3 = (bf16[1024,128]{1,0:T(8,128)(2,1)S(1)}, bf16[1024,128]{1,0:T(8,128)(2,1)}, u32[]{:S(2)}, u32[]{:S(2)}) collective-permute-start(bf16[1024,128]{1,0:T(8,128)(2,1)S(1)} %bitcast.18), channel_id=1, source_target_pairs={{0,8},{8,0},{1,9},{9,1},{2,10},{10,2},{3,11},{11,3},{4,12},{12,4},... | collective-permute-start | bytes 786440 | tf_op jit(solution)/shard_map/sibling/ppermute | solution.py:264
  79.6 5.9 %all-to-all-done.4.own_ref.left_ref = f32[32,4,640]{2,1,0:T(4,128)S(1)} async-done(((f32[32,4,640]{2,1,0:T(4,128)}), f32[32,4,640]{2,1,0:T(4,128)S(1)}, u32[]{:S(2)}, u32[]{:S(2)}) %all-to-all-start.4) | async-done | bytes 327712 | tf_op jit(solution)/shard_map/left_sum/all_to_all | solution.py:274
  85.5 3.1 %token_products.1 = f32[8,32,128]{2,1,0:T(8,128)} custom-call(f32[32,4,640]{2,1,0:T(4,128)S(1)} %all-to-all-done.4.own_ref.left_ref, bf16[128,5120]{1,0:T(8,128)(2,1)S(1)} %bitcast.16, bf16[128,5120]{1,0:T(8,128)(2,1)} %collective-permute-done.1.sibling_ref), custom_call_target="tpu_custom_call" | custom-call | flops 125829120 | bytes 4194304 | tf_op jit(solution)/shard_map/token_products/pallas_call | solution.py:25
  88.6 3.4 %all-to-all-start.5 = ((f32[8,32,128]{2,1,0:T(8,128)}), f32[8,32,128]{2,1,0:T(8,128)S(1)}, u32[]{:S(2)}, u32[]{:S(2)}) async-start(f32[8,32,128]{2,1,0:T(8,128)} %token_products.1), calls=%async_computation.5 | async-start | bytes 262144 | tf_op jit(solution)/shard_map/token_products/all_to_all | solution.py:279
  92.0 6.4 %collective-permute-start = (f32[32,4,640]{2,1,0:T(4,128)S(1)}, f32[32,4,640]{2,1,0:T(4,128)S(1)}, u32[]{:S(2)}, u32[]{:S(2)}) collective-permute-start(f32[32,4,640]{2,1,0:T(4,128)S(1)} %all-to-all-done.4.own_ref.left_ref), channel_id=1, source_target_pairs={{0,8},{8,0},{1,9},{9,1},{2,10},{10,2},{3,11},{11,3},{4,12},{12,4},... | collective-permute-start | bytes 983048 | tf_op jit(solution)/shard_map/orthonormal/ppermute | solution.py:285
  98.3 1.9 %residual_right.1.base_ref = f32[16,128]{1,0:T(8,128)S(1)} custom-call(f32[32,4,640]{2,1,0:T(4,128)S(1)} %all-to-all-done.4.own_ref.left_ref, bf16[5120,128]{1,0:T(8,128)(2,1)S(1)} %bitcast.12, bf16[5120,128]{1,0:T(8,128)(2,1)} %collective-permute-done.2.sibling_ref), custom_call_target="tpu_custom_call" | custom-call | flops 125829120 | bytes 4194304 | tf_op jit(solution)/shard_map/residual_right/pallas_call | solution.py:25
  100.2 0.9 all-to-all-done.5.tokens_ref
  101.2 2.0 %right_terms.1 = f32[32,16,128]{2,1,0:T(8,128)} custom-call(f32[8,32,128]{2,1,0:T(8,128)S(1)} %all-to-all-done.5.tokens_ref, f32[16,128]{1,0:T(8,128)S(1)} %residual_right.1.base_ref, bf16[1024,128]{1,0:T(8,128)(2,1)S(1)} %bitcast.19, bf16[1024,128]{1,0:T(8,128)(2,1)} %collective-permute-done.3.sibling_ref), custom_call_target="tpu_custom_call" | custom-call | flops 25165824 | bytes 524288 | tf_op jit(solution)/shard_map/right_terms/pallas_call | solution.py:25
  103.2 6.1 %all-to-all-start.6 = ((f32[32,16,128]{2,1,0:T(8,128)}), f32[32,16,128]{2,1,0:T(8,128)S(1)}, u32[]{:S(2)}, u32[]{:S(2)}) async-start(f32[32,16,128]{2,1,0:T(8,128)} %right_terms.1), calls=%async_computation.6 | async-start | bytes 524288 | tf_op jit(solution)/shard_map/right_sum/all_to_all | solution.py:291
  109.3 4.6 %orthonormal.1 = (bf16[96,5120]{1,0:T(8,128)(2,1)S(1)}, f32[32,640]{1,0:T(8,128)}, f32[32,32]{1,0:T(8,128)S(1)}) custom-call(s32[1]{0:T(128)} %bitcast.core_ref, s32[1]{0:T(128)} %bitcast.1.at_ref, f32[32,4,640]{2,1,0:T(4,128)S(1)} %all-to-all-done.4.own_ref.left_ref, f32[32,4,640]{2,1,0:T(4,128)S(1)} %collective-permute-done.other_ref), custom_call_target="tpu_custom_call" | custom-call | flops 4294967296 | bytes 4194304 | tf_op jit(solution)/shard_map/orthonormal/pallas_call | solution.py:25
  113.9 5.0 %all-to-all-done.6.in_ref = f32[32,16,128]{2,1,0:T(8,128)S(1)} async-done(((f32[32,16,128]{2,1,0:T(8,128)}), f32[32,16,128]{2,1,0:T(8,128)S(1)}, u32[]{:S(2)}, u32[]{:S(2)}) %all-to-all-start.6) | async-done | bytes 262176 | tf_op jit(solution)/shard_map/right_sum/all_to_all | solution.py:291
  118.9 7.4 %collective-permute-start.4 = (f32[16,128]{1,0:T(8,128)S(1)}, f32[16,128]{1,0:T(8,128)S(1)}, u32[]{:S(2)}, u32[]{:S(2)}) collective-permute-start(f32[16,128]{1,0:T(8,128)S(1)} %right_sum.1.own_ref), channel_id=1, source_target_pairs={{0,8},{8,0},{1,9},{9,1},{2,10},{10,2},{3,11},{11,3},{4,12},{12,4},... | collective-permute-start | bytes 24584 | tf_op jit(solution)/shard_map/right_sum/ppermute | solution.py:310
  126.4 0.8 collective-permute-done.4.other_ref
  127.2 1.2 right_and_base.1
  128.4 1.6 %copy-done.2 = f32[5120,128]{1,0:T(8,128)} copy-done((f32[5120,128]{1,0:T(8,128)}, f32[5120,128]{1,0:T(8,128)S(1)}, u32[]{:S(2)}) %copy-start.2) | copy-done | bytes 2621464
  130.0 0.7 copy-done.4
  130.7 5.7 %all-gather.3.cloned.1.call-done = bf16[1,1024,5120]{2,1,0:T(8,128)(2,1)} async-done(((bf16[1,128,5120]{2,1,0:T(8,128)(2,1)}), bf16[1,1024,5120]{2,1,0:T(8,128)(2,1)}) %all-gather.3.cloned.1.call-update) | async-done | bytes 10485776 | tf_op jit(solution)/shard_map/gather_activations/all_gather | solution.py:255
  136.3 6.6 %residual_out.1 = bf16[5120,128]{1,0:T(8,128)(2,1)} custom-call(bf16[128,1024]{1,0:T(8,128)(2,1)} %copy-done.4, bf16[1024,5120]{1,0:T(8,128)(2,1)} %bitcast.23, f32[5120,128]{1,0:T(8,128)} %copy-done.2), custom_call_target="tpu_custom_call" | custom-call | flops 2147483648 | bytes 16777216 | tf_op jit(solution)/shard_map/residual_out/pallas_call | solution.py:319
  (18 shorter events, 0.9 us)
Async XLA Ops:
  7.2 0.8 copy-start.5
  7.2 1.0 copy-start.3
  7.2 9.5 %copy-start = (bf16[1,5120,128]{2,1,0:T(8,128)(2,1)S(1)}, bf16[1,5120,128]{2,1,0:T(8,128)(2,1)}, u32[]{:S(2)}) copy-start(bf16[1,5120,128]{2,1,0:T(8,128)(2,1)} %param.6) | copy-start | bytes 3932164
  7.2 129.1 %all-gather.3.cloned.1.call-start = ((), (), s32[]{:S(2)}) async-start(), calls=%async_computation.7 | async-start | bytes 11796480 | tf_op jit(solution)/shard_map/gather_activations/all_gather | solution.py:255
  8.1 16.7 %copy-start.1 = (bf16[1,128,5120]{2,1,0:T(8,128)(2,1)S(1)}, bf16[1,128,5120]{2,1,0:T(8,128)(2,1)}, u32[]{:S(2)}) copy-start(bf16[1,128,5120]{2,1,0:T(8,128)(2,1)} %param.4) | copy-start | bytes 3932164
  9.1 15.8 %all-to-all-start = ((f32[8,32,128]{2,1,0:T(8,128)}), f32[8,32,128]{2,1,0:T(8,128)}, u32[]{:S(2)}, u32[]{:S(2)}) async-start(f32[8,32,128]{2,1,0:T(8,128)} %token_terms.1), calls=%async_computation | async-start | bytes 262144 | tf_op jit(solution)/shard_map/token_terms/all_to_all | solution.py:259
  35.0 21.2 %all-to-all-start.2 = ((f32[32,4,640]{2,1,0:T(4,128)}), f32[32,4,640]{2,1,0:T(4,128)S(1)}, u32[]{:S(2)}, u32[]{:S(2)}) async-start(f32[32,4,640]{2,1,0:T(4,128)} %left_sum.3), calls=%async_computation.2 | async-start | bytes 655360 | tf_op jit(solution)/shard_map/left_sum/all_to_all | solution.py:270
  45.7 33.8 %collective-permute-start.1 = (bf16[128,5120]{1,0:T(8,128)(2,1)S(1)}, bf16[128,5120]{1,0:T(8,128)(2,1)}, u32[]{:S(2)}, u32[]{:S(2)}) collective-permute-start(bf16[128,5120]{1,0:T(8,128)(2,1)S(1)} %bitcast.15), channel_id=1, source_target_pairs={{0,8},{8,0},{1,9},{9,1},{2,10},{10,2},{3,11},{11,3},{4,12},{12,4},... | collective-permute-start | bytes 3932168 | tf_op jit(solution)/shard_map/sibling/ppermute | solution.py:264
  48.3 50.0 %collective-permute-start.2 = (bf16[5120,128]{1,0:T(8,128)(2,1)S(1)}, bf16[5120,128]{1,0:T(8,128)(2,1)}, u32[]{:S(2)}, u32[]{:S(2)}) collective-permute-start(bf16[5120,128]{1,0:T(8,128)(2,1)S(1)} %bitcast.11), channel_id=1, source_target_pairs={{0,8},{8,0},{1,9},{9,1},{2,10},{10,2},{3,11},{11,3},{4,12},{12,4},... | collective-permute-start | bytes 3932168 | tf_op jit(solution)/shard_map/sibling/ppermute | solution.py:264
  67.6 17.8 %all-to-all-start.4 = ((f32[32,4,640]{2,1,0:T(4,128)}), f32[32,4,640]{2,1,0:T(4,128)S(1)}, u32[]{:S(2)}, u32[]{:S(2)}) async-start(f32[32,4,640]{2,1,0:T(4,128)} %left_sum.5), calls=%async_computation.4 | async-start | bytes 655360 | tf_op jit(solution)/shard_map/left_sum/all_to_all | solution.py:274
  75.5 24.8 %collective-permute-start.3 = (bf16[1024,128]{1,0:T(8,128)(2,1)S(1)}, bf16[1024,128]{1,0:T(8,128)(2,1)}, u32[]{:S(2)}, u32[]{:S(2)}) collective-permute-start(bf16[1024,128]{1,0:T(8,128)(2,1)S(1)} %bitcast.18), channel_id=1, source_target_pairs={{0,8},{8,0},{1,9},{9,1},{2,10},{10,2},{3,11},{11,3},{4,12},{12,4},... | collective-permute-start | bytes 786440 | tf_op jit(solution)/shard_map/sibling/ppermute | solution.py:264
  88.6 12.6 %all-to-all-start.5 = ((f32[8,32,128]{2,1,0:T(8,128)}), f32[8,32,128]{2,1,0:T(8,128)S(1)}, u32[]{:S(2)}, u32[]{:S(2)}) async-start(f32[8,32,128]{2,1,0:T(8,128)} %token_products.1), calls=%async_computation.5 | async-start | bytes 262144 | tf_op jit(solution)/shard_map/token_products/all_to_all | solution.py:279
  92.0 17.3 %collective-permute-start = (f32[32,4,640]{2,1,0:T(4,128)S(1)}, f32[32,4,640]{2,1,0:T(4,128)S(1)}, u32[]{:S(2)}, u32[]{:S(2)}) collective-permute-start(f32[32,4,640]{2,1,0:T(4,128)S(1)} %all-to-all-done.4.own_ref.left_ref), channel_id=1, source_target_pairs={{0,8},{8,0},{1,9},{9,1},{2,10},{10,2},{3,11},{11,3},{4,12},{12,4},... | collective-permute-start | bytes 983048 | tf_op jit(solution)/shard_map/orthonormal/ppermute | solution.py:285
  103.2 15.7 %all-to-all-start.6 = ((f32[32,16,128]{2,1,0:T(8,128)}), f32[32,16,128]{2,1,0:T(8,128)S(1)}, u32[]{:S(2)}, u32[]{:S(2)}) async-start(f32[32,16,128]{2,1,0:T(8,128)} %right_terms.1), calls=%async_computation.6 | async-start | bytes 524288 | tf_op jit(solution)/shard_map/right_sum/all_to_all | solution.py:291
  118.9 8.2 %collective-permute-start.4 = (f32[16,128]{1,0:T(8,128)S(1)}, f32[16,128]{1,0:T(8,128)S(1)}, u32[]{:S(2)}, u32[]{:S(2)}) collective-permute-start(f32[16,128]{1,0:T(8,128)S(1)} %right_sum.1.own_ref), channel_id=1, source_target_pairs={{0,8},{8,0},{1,9},{9,1},{2,10},{10,2},{3,11},{11,3},{4,12},{12,4},... | collective-permute-start | bytes 24584 | tf_op jit(solution)/shard_map/right_sum/ppermute | solution.py:310
  128.4 1.6 %copy-start.2 = (f32[5120,128]{1,0:T(8,128)}, f32[5120,128]{1,0:T(8,128)S(1)}, u32[]{:S(2)}) copy-start(f32[5120,128]{1,0:T(8,128)S(1)} %get-tuple-element.26.base_ref) | copy-start | bytes 7864324
  130.0 0.7 copy-start.4
Sparse Core Ops, SparseCore 0:
  10.1 126.1 all-gather.2
